TPU v7x, 32 devices: a whole 2x2x4 slice. The times are simulated.
32 devices in a mesh: ky: 8 (over y, x, core), kz: 4 (over z).
Axes of the slice: x: 2, y: 2, z: 4, core: 2. Of those that a mesh axis runs over, the one named last changes fastest.
Arguments:
- fields: bfloat16 [4, 2, 8, 1024, 1024], P(None, None, None, 'ky', 'kz'), may hold values from -6 to 6
- offsets: int32 [8], replicated, may hold values from 0 to 1023, as said below
Outputs:
- velocity_field: bfloat16 [3, 2, 8, 1024, 1024], P(None, None, 'ky', 'kz')
- scalar_spectrum: bfloat16 [2, 8, 1024, 1024], P(None, None, 'ky', 'kz')
Inputs may be any that keep to these rules, and one draw needn't show every extreme that they name: `offsets`: ky roll of each kx plane; both ends are taken in every draw.
All inputs are finite; a program needn't handle non-finite values.
Results may differ from a plain program's by a relative error of at most 0.0059.
Values may be sent and summed in bfloat16 or wider, within the bound.
No kernel may reach another device: no remote copies, remote signals or barrier semaphores. Data moves between devices by JAX's collectives and lax.ppermute only.
A program may use at most 128 MiB of HBM per device.

v0:
```python
import functools
import math

import jax
import jax.numpy as jnp
import ml_dtypes
import numpy as np
from jax import lax
from jax.experimental import pallas as pl
from jax.experimental.pallas import tpu as pltpu
from jax.sharding import PartitionSpec as P

VMEM_LIMIT = 64 * 1024 * 1024
COST = pl.CostEstimate(flops=0, bytes_accessed=0, transcendentals=0)
HIGH = pl.CostEstimate(flops=40_000_000_000, bytes_accessed=0, transcendentals=0)


def tables(length):
    counter = np.arange(length, dtype=np.int64)
    product = (counter[:, None] * counter[None, :]) % length
    angles = product.astype(np.float32) * np.float32(2.0 * math.pi / length)
    return (np.cos(angles).astype(ml_dtypes.bfloat16), np.sin(angles).astype(ml_dtypes.bfloat16))


def y_table(length, targets):
    order = np.concatenate([np.arange(0, length, 2), np.arange(1, length, 2)])
    parts = [table[: length // 2, order].reshape(targets // 2, length // targets, length) for table in tables(length)]
    return jnp.asarray(np.concatenate(parts, axis=1))


def z_table(length, tile):
    half = length // 2
    order = np.concatenate([np.arange(0, length, 2), np.arange(1, length, 2)])
    parts = [table[order, :half].reshape(length, half // tile, tile).swapaxes(0, 1) for table in tables(length)]
    return jnp.asarray(np.concatenate(parts, axis=2))


def dot(left, right):
    return lax.dot_general(left, right, (((1,), (0,)), ((), ())), preferred_element_type=jnp.float32)


def shift_rows(slots, offset, store, parity):
    count, rows, _ = slots[0].shape
    whole, rest = offset // rows, offset % rows
    to_row = lax.broadcasted_iota(jnp.int32, (rows, 2 * rows), 0)
    if parity:
        to_row = jnp.where(to_row < rows // 2, 2 * to_row, 2 * to_row - (rows - 1))
    from_row = lax.broadcasted_iota(jnp.int32, (rows, 2 * rows), 1)
    pick = jnp.where(from_row == rows + to_row - rest, 1.0, 0.0).astype(jnp.bfloat16)
    for block in range(count):
        here = lax.rem(block - whole + count, count)
        before = lax.rem(block - whole - 1 + 2 * count, count)
        for part, slot in enumerate(slots):
            window = jnp.concatenate([slot[before], slot[here]], axis=0)
            store(block, part, dot(pick, window).astype(jnp.bfloat16))


def y_kernel(targets, halves, place_ref, blocks_hbm, table_hbm, *refs):
    count = targets * halves
    outs, (blocks, table, rolled, pieces, sems, out_sems) = refs[:count], refs[count:]
    planes, _, rows, columns = blocks.shape
    length = planes * rows
    y_rows = length // targets
    half_rows = y_rows // halves
    pairs = targets // 2
    factor = 1.0 / math.sqrt(length)

    load = pltpu.make_async_copy(blocks_hbm.at[:, pl.ds(0, 2)], blocks, sems.at[pairs])
    load.start()
    loads = []
    for step in range(pairs):
        wanted = lax.rem(place_ref[1] + step, pairs)
        loads.append(pltpu.make_async_copy(table_hbm.at[wanted], table.at[step], sems.at[step]))
        loads[-1].start()
    load.wait()

    def store(block, part, values):
        lanes = pl.ds(part * columns, columns)
        for odd in range(2):
            start = odd * (length // 2) + block * (rows // 2)
            rolled[pl.ds(start, rows // 2), lanes] = values[odd * (rows // 2) : (odd + 1) * (rows // 2)]

    shift_rows([blocks.at[:, part] for part in range(2)], place_ref[0], store, parity=True)

    def product(step, start):
        both = dot(table[step, :, pl.ds(start, length // 2)], rolled[pl.ds(start, length // 2), :])
        real = both[:y_rows, :columns] - both[y_rows:, columns:]
        imag = both[y_rows:, :columns] + both[:y_rows, columns:]
        return real, imag

    stores = []
    for step in range(pairs):
        loads[step].wait()
        sign = jnp.where(lax.rem(place_ref[1] + step, targets) < pairs, factor, -factor)
        even = product(step, 0)
        odd = product(step, length // 2)
        for part in range(2):
            from_even, from_odd = even[part] * factor, odd[part] * sign
            pieces[step, part] = (from_even + from_odd).astype(jnp.bfloat16)
            pieces[step + pairs, part] = (from_even - from_odd).astype(jnp.bfloat16)
        for index in (step, step + pairs):
            for half in range(halves):
                number = half * targets + index
                stores.append(
                    pltpu.make_async_copy(
                        pieces.at[index, :, pl.ds(half * half_rows, half_rows)], outs[number], out_sems.at[number]
                    )
                )
                stores[-1].start()
    for copy in stores:
        copy.wait()


IN_HBM = pl.BlockSpec(memory_space=pltpu.HBM)
IN_SMEM = pl.BlockSpec(memory_space=pltpu.SMEM)


def y_transform(blocks, place, table, targets, halves, cost):
    planes, _, rows, columns = blocks.shape
    length = planes * rows
    y_rows = length // targets
    count = targets * halves
    return pl.pallas_call(
        functools.partial(y_kernel, targets, halves),
        out_shape=[jax.ShapeDtypeStruct((2, y_rows // halves, columns), jnp.bfloat16)] * count,
        in_specs=[IN_SMEM, IN_HBM, IN_HBM],
        out_specs=[IN_HBM] * count,
        scratch_shapes=[
            pltpu.VMEM((planes, 2, rows, columns), jnp.bfloat16),
            pltpu.VMEM(table.shape, jnp.bfloat16),
            pltpu.VMEM((length, 2 * columns), jnp.bfloat16),
            pltpu.VMEM((targets, 2, y_rows, columns), jnp.bfloat16),
            pltpu.SemaphoreType.DMA((targets // 2 + 1,)),
            pltpu.SemaphoreType.DMA((count,)),
        ],
        compiler_params=pltpu.CompilerParams(vmem_limit_bytes=VMEM_LIMIT),
        cost_estimate=cost,
        name="y_transform",
    )(place, blocks, table)


def z_kernel(layout, targets, component, first_row, place_ref, *refs):
    pieces, table_hbm = refs[: len(layout)], refs[len(layout)]
    field, joined, split, table, out, sems, table_sems, out_sems = refs[-8:]
    rows = joined.shape[0] // 2
    tiles, length, tile = table.shape[0], table.shape[1], table.shape[2] // 2
    columns = length // targets
    factor = 1.0 / math.sqrt(length)

    def place_piece(number):
        piece, (behind, row, lane) = pieces[number], layout[number]
        source = lax.rem(place_ref[1] + targets - behind, targets)
        _, some_rows, some_columns = piece.shape
        start = pl.multiple_of(source * columns, columns) + lane
        return [
            pltpu.make_async_copy(
                piece.at[part],
                joined.at[pl.ds(part * rows + row, some_rows), pl.ds(start, some_columns)],
                sems.at[number, part],
            )
            for part in range(2)
        ]

    loads = [copy for number in range(len(layout)) for copy in place_piece(number)]
    for copy in loads:
        copy.start()
    tables = [pltpu.make_async_copy(table_hbm.at[step], table.at[step], table_sems.at[step]) for step in range(tiles)]
    for copy in tables:
        copy.start()

    lane = lax.broadcasted_iota(jnp.int32, (columns, columns), 1)
    wanted = jnp.where(lane < columns // 2, 2 * lane, 2 * lane - (columns - 1))
    pick = jnp.where(lax.broadcasted_iota(jnp.int32, (columns, columns), 0) == wanted, 1.0, 0.0).astype(jnp.bfloat16)
    for copy in loads:
        copy.wait()
    for source in range(targets):
        parted = dot(joined[:, pl.ds(source * columns, columns)], pick).astype(jnp.bfloat16)
        split[:, pl.ds(source * columns // 2, columns // 2)] = parted[:, : columns // 2]
        split[:, pl.ds((length + source * columns) // 2, columns // 2)] = parted[:, columns // 2 :]

    def product(step, start):
        lanes = pl.ds(start, length // 2)
        both = dot(split[:, lanes], table[step, lanes, :])
        return both[:rows, :tile] - both[rows:, tile:], both[:rows, tile:] + both[rows:, :tile]

    stores = []
    for step in range(tiles):
        tables[step].wait()
        even = product(step, 0)
        odd = product(step, length // 2)
        for part in range(2):
            out[step, part] = ((even[part] + odd[part]) * factor).astype(jnp.bfloat16)
            out[step + tiles, part] = ((even[part] - odd[part]) * factor).astype(jnp.bfloat16)
        for number in (step, step + tiles):
            stores.append(
                pltpu.make_async_copy(
                    out.at[number],
                    field.at[component, :, 0, pl.ds(first_row, rows), pl.ds(number * tile, tile)],
                    out_sems.at[number],
                )
            )
            stores[-1].start()
    for copy in stores:
        copy.wait()


def z_transform(pieces, layout, place, table, targets, component, first_row, field, shape, cost):
    rows = max(row + piece.shape[1] for piece, (_, row, _) in zip(pieces, layout))
    tiles, length, _ = table.shape
    through = [] if field is None else [field]
    return pl.pallas_call(
        functools.partial(z_kernel, layout, targets, component, first_row),
        out_shape=jax.ShapeDtypeStruct(shape, jnp.bfloat16),
        in_specs=[IN_SMEM] + [IN_HBM] * (len(pieces) + 1 + len(through)),
        out_specs=IN_HBM,
        scratch_shapes=[
            pltpu.VMEM((2 * rows, length), jnp.bfloat16),
            pltpu.VMEM((2 * rows, length), jnp.bfloat16),
            pltpu.VMEM(table.shape, jnp.bfloat16),
            pltpu.VMEM((2 * tiles, 2, rows, length // tiles // 2), jnp.bfloat16),
            pltpu.SemaphoreType.DMA((len(pieces), 2)),
            pltpu.SemaphoreType.DMA((tiles,)),
            pltpu.SemaphoreType.DMA((2 * tiles,)),
        ],
        input_output_aliases={} if field is None else {len(pieces) + 2: 0},
        compiler_params=pltpu.CompilerParams(vmem_limit_bytes=VMEM_LIMIT),
        cost_estimate=cost,
        name="z_transform",
    )(place, *pieces, table, *through)


def roll_kernel(numbers, place_ref, *refs):
    slots = refs[: len(numbers)]
    out_hbm, blocks, out, sems, out_sem = refs[len(numbers) :]
    loads = [
        pltpu.make_async_copy(slot.at[:, number], blocks.at[part], sems.at[part])
        for part, (slot, number) in enumerate(zip(slots, numbers))
    ]
    for copy in loads:
        copy.start()
    for copy in loads:
        copy.wait()

    def store(block, part, values):
        out[block, part] = values

    shift_rows([blocks.at[part] for part in range(len(numbers))], place_ref[0], store, parity=False)
    copy = pltpu.make_async_copy(out, out_hbm, out_sem.at[0])
    copy.start()
    copy.wait()


def roll_planes(place, *slots):
    count, _, rows, columns = slots[0][0].shape
    return pl.pallas_call(
        functools.partial(roll_kernel, [number for _, number in slots]),
        out_shape=jax.ShapeDtypeStruct((count, len(slots), rows, columns), jnp.bfloat16),
        in_specs=[IN_SMEM] + [IN_HBM] * len(slots),
        out_specs=IN_HBM,
        scratch_shapes=[
            pltpu.VMEM((len(slots), count, rows, columns), jnp.bfloat16),
            pltpu.VMEM((count, len(slots), rows, columns), jnp.bfloat16),
            pltpu.SemaphoreType.DMA((len(slots),)),
            pltpu.SemaphoreType.DMA((1,)),
        ],
        compiler_params=pltpu.CompilerParams(vmem_limit_bytes=VMEM_LIMIT),
        cost_estimate=COST,
        name="roll_planes",
    )(place, *[blocks for blocks, _ in slots])


def restack_kernel(steps, from_hbm, out_hbm, held, sems, out_sems):
    loads = [pltpu.make_async_copy(from_hbm.at[source], held.at[part], sems.at[part]) for part, (source, _) in enumerate(steps)]
    for copy in loads:
        copy.start()
    stores = []
    for part, (_, target) in enumerate(steps):
        loads[part].wait()
        stores.append(pltpu.make_async_copy(held.at[part], out_hbm.at[target], out_sems.at[part]))
        stores[-1].start()
    for copy in stores:
        copy.wait()


def restack(array, steps, shape, name):
    return pl.pallas_call(
        functools.partial(restack_kernel, steps),
        out_shape=jax.ShapeDtypeStruct(shape, array.dtype),
        in_specs=[IN_HBM],
        out_specs=IN_HBM,
        scratch_shapes=[
            pltpu.VMEM((len(steps), array.shape[-3] if array.ndim == 5 else array.shape[0], *array.shape[-2:]), array.dtype),
            pltpu.SemaphoreType.DMA((len(steps),)),
            pltpu.SemaphoreType.DMA((len(steps),)),
        ],
        compiler_params=pltpu.CompilerParams(vmem_limit_bytes=VMEM_LIMIT),
        cost_estimate=COST,
        name=name,
    )(array)


def by_plane(fields, *slots):
    _, _, planes, rows, columns = fields.shape
    steps = [(slot, (slice(None), number)) for number, slot in enumerate(slots)]
    return restack(fields, steps, (planes, len(slots), rows, columns), "by_plane")


def by_part(planes):
    count, parts, rows, columns = planes.shape
    steps = [((slice(None), part), (part,)) for part in range(parts)]
    return restack(planes, steps, (parts, count, rows, columns), "by_part")


def nothing_kernel(*refs):
    pass


def after(array, *others, cost=COST):
    anywhere = IN_HBM
    return pl.pallas_call(
        nothing_kernel,
        out_shape=jax.ShapeDtypeStruct(array.shape, array.dtype),
        in_specs=[anywhere] * (1 + len(others)),
        out_specs=anywhere,
        input_output_aliases={0: 0},
        compiler_params=pltpu.CompilerParams(vmem_limit_bytes=VMEM_LIMIT),
        cost_estimate=cost,
        name="after",
    )(array, *others)


def exchange(blocks):
    return lax.all_to_all(blocks, "ky", 0, 0, tiled=True)


def along_z(others):
    targets = len(others) + 1
    return [
        lax.ppermute(piece, "kz", [(i, (i + step) % targets) for i in range(targets)])
        for step, piece in enumerate(others, 1)
    ]


def shards(fields, offsets):
    components = fields.shape[0] - 1
    targets = lax.axis_size("kz")
    assert fields.shape[2] == lax.axis_size("ky") and components == 3
    place = jnp.stack([offsets[lax.axis_index("ky")], lax.axis_index("kz").astype(jnp.int32)])
    y_rows = fields.shape[3] * lax.axis_size("ky") // targets
    shape = (components, 2, 1, y_rows, fields.shape[4] * targets)
    ky_table = y_table(y_rows * targets, targets)
    kz_table = z_table(shape[-1], 256)

    def y_of(blocks, halves, cost=COST):
        pieces = y_transform(blocks, place, ky_table, targets, halves, cost)
        groups = [pieces[half * targets : (half + 1) * targets] for half in range(halves)]
        return [[group[0], *along_z(group[1:])] for group in groups]

    def z_of(groups, starts, component, first_row, field, cost=COST):
        layout = [(behind, *start) for start in starts for behind in range(targets)]
        pieces = [piece for group in groups for piece in group]
        return z_transform(pieces, layout, place, kz_table, targets, component, first_row, field, shape, cost)

    by_rows = [(0, 0), (y_rows // 2, 0)]
    blocks0 = exchange(by_plane(fields, (0, 0), (0, 1)))
    blocks1 = exchange(after(by_plane(fields, (1, 0), (1, 1), (components, 0), (components, 1)), blocks0))
    pieces0 = y_of(blocks0, 1, HIGH)[0]
    pieces1 = y_of(blocks1, 1)[0]
    third = after(by_plane(fields, (2, 0), (2, 1)), blocks1, *pieces0[1:])
    blocks2 = exchange(after(third, pieces1[0], cost=HIGH))
    field = z_of([pieces0], by_rows[:1], 0, 0, None, HIGH)
    pieces2, pieces3 = y_of(after(blocks2, field), 2)
    plane = roll_planes(place, (blocks1, 2), (blocks1, 3))
    scalar = by_part(exchange(plane))
    field = z_of([pieces1], by_rows[:1], 1, 0, field)
    pieces2[0] = after(pieces2[0], plane, cost=HIGH)
    field = z_of([pieces2], by_rows[:1], 2, 0, field, HIGH)
    field = z_of([pieces3], by_rows[:1], 2, y_rows // 2, field)
    return (field, scalar)


def solution(mesh):
    placed = (P(None, None, None, "ky", "kz"), P())
    return jax.shard_map(
        shards,
        mesh=mesh,
        in_specs=placed,
        out_specs=(P(None, None, "ky", "kz", None), P(None, None, "ky", "kz")),
        check_vma=False,
    )
```

profile of v0, /device:TPU:11, one launch (start us, length us, event | category | flops | bytes accessed | tf_op | source)
XLA Modules:
  0.0 117.8 jit_solution(4139922526599346665)
XLA Ops:
  0.6 2.0 %by_plane.5 = bf16[8,2,128,256]{3,2,1,0:T(8,128)(2,1)} custom-call(bf16[4,2,8,128,256]{4,3,2,1,0:T(8,128)(2,1)} %from_hbm.5), custom_call_target="tpu_custom_call" | custom-call | tf_op jit(solution)/shard_map/by_plane/pallas_call | solution.py:286
  2.7 5.0 %all-to-all-start = ((bf16[8,2,128,256]{3,2,1,0:T(8,128)(2,1)}), bf16[8,2,128,256]{3,2,1,0:T(8,128)(2,1)}, u32[]{:S(2)}, u32[]{:S(2)}) async-start(bf16[8,2,128,256]{3,2,1,0:T(8,128)(2,1)} %by_plane.5), calls=%async_computation | async-start | bytes 2097152 | tf_op jit(solution)/shard_map/all_to_all | solution.py:333
  7.7 2.4 %by_plane.4.refs_0_ = bf16[8,4,128,256]{3,2,1,0:T(8,128)(2,1)} custom-call(bf16[4,2,8,128,256]{4,3,2,1,0:T(8,128)(2,1)} %from_hbm.5), custom_call_target="tpu_custom_call" | custom-call | tf_op jit(solution)/shard_map/by_plane/pallas_call | solution.py:286
  12.6 9.0 %all-to-all-done.refs_1_.blocks_hbm = bf16[8,2,128,256]{3,2,1,0:T(8,128)(2,1)} async-done(((bf16[8,2,128,256]{3,2,1,0:T(8,128)(2,1)}), bf16[8,2,128,256]{3,2,1,0:T(8,128)(2,1)}, u32[]{:S(2)}, u32[]{:S(2)}) %all-to-all-start) | async-done | bytes 1048608 | tf_op jit(solution)/shard_map/all_to_all | solution.py:333
  21.6 5.8 %all-to-all-start.1 = ((bf16[8,4,128,256]{3,2,1,0:T(8,128)(2,1)}), bf16[8,4,128,256]{3,2,1,0:T(8,128)(2,1)}, u32[]{:S(2)}, u32[]{:S(2)}) async-start(bf16[8,4,128,256]{3,2,1,0:T(8,128)(2,1)} %after.5), calls=%async_computation.1 | async-start | bytes 4194304 | tf_op jit(solution)/shard_map/all_to_all | solution.py:333
  27.4 4.6 %y_transform.3 = (bf16[2,256,256]{2,1,0:T(8,128)(2,1)}, bf16[2,256,256]{2,1,0:T(8,128)(2,1)}, bf16[2,256,256]{2,1,0:T(8,128)(2,1)}, bf16[2,256,256]{2,1,0:T(8,128)(2,1)}) custom-call(s32[2]{0:T(128)} %pad_add_fusion.place_ref, bf16[8,2,128,256]{3,2,1,0:T(8,128)(2,1)} %all-to-all-done.refs_1_.blocks_hbm, bf16[2,512,1024]{2,1,0:T(8,128)(2,1)} %constant.17.clone.table_hbm), custom_call_target="tpu_custom_call" | custom-call | flops 40000000000 | tf_op jit(solution)/shard_map/y_transform/pallas_call | solution.py:123
  35.9 2.0 %by_plane.3.refs_0_ = bf16[8,2,128,256]{3,2,1,0:T(8,128)(2,1)} custom-call(bf16[4,2,8,128,256]{4,3,2,1,0:T(8,128)(2,1)} %from_hbm.5), custom_call_target="tpu_custom_call" | custom-call | tf_op jit(solution)/shard_map/by_plane/pallas_call | solution.py:286
  38.0 14.7 %all-to-all-done.1.refs_1_.blocks_hbm.refs_0_ = bf16[8,4,128,256]{3,2,1,0:T(8,128)(2,1)} async-done(((bf16[8,4,128,256]{3,2,1,0:T(8,128)(2,1)}), bf16[8,4,128,256]{3,2,1,0:T(8,128)(2,1)}, u32[]{:S(2)}, u32[]{:S(2)}) %all-to-all-start.1) | async-done | bytes 2097184 | tf_op jit(solution)/shard_map/all_to_all | solution.py:333
  52.6 4.7 %y_transform.4 = (bf16[2,256,256]{2,1,0:T(8,128)(2,1)}, bf16[2,256,256]{2,1,0:T(8,128)(2,1)}, bf16[2,256,256]{2,1,0:T(8,128)(2,1)}, bf16[2,256,256]{2,1,0:T(8,128)(2,1)}) custom-call(s32[2]{0:T(128)} %pad_add_fusion.place_ref, bf16[8,4,128,256]{3,2,1,0:T(8,128)(2,1)} %all-to-all-done.1.refs_1_.blocks_hbm.refs_0_, bf16[2,512,1024]{2,1,0:T(8,128)(2,1)} %constant.17.clone.table_hbm), custom_call_target="tpu_custom_call" | custom-call | tf_op jit(solution)/shard_map/y_transform/pallas_call | solution.py:123
  58.4 4.7 %all-to-all-start.2 = ((bf16[8,2,128,256]{3,2,1,0:T(8,128)(2,1)}), bf16[8,2,128,256]{3,2,1,0:T(8,128)(2,1)}, u32[]{:S(2)}, u32[]{:S(2)}) async-start(bf16[8,2,128,256]{3,2,1,0:T(8,128)(2,1)} %after.7), calls=%async_computation.2 | async-start | bytes 2097152 | tf_op jit(solution)/shard_map/all_to_all | solution.py:333
  64.4 4.9 %z_transform.4.refs_1_.refs_5_ = bf16[3,2,1,256,1024]{4,3,2,1,0:T(8,128)(2,1)} custom-call(s32[2]{0:T(128)} %pad_add_fusion.place_ref, bf16[2,256,256]{2,1,0:T(8,128)(2,1)} %get-tuple-element.22.refs_0_, bf16[2,256,256]{2,1,0:T(8,128)(2,1)} %collective-permute-done.refs_2_.refs_1_, bf16[2,256,256]{2,1,0:T(8,128)(2,1)} %collective-permute-done.1.refs_3_.refs_2_, ...), custom_call_target="tpu_custom_call" | custom-call | flops 40000000000 | tf_op jit(solution)/shard_map/z_transform/pallas_call | solution.py:211
  70.4 1.5 %collective-permute-start.11 = (bf16[2,256,256]{2,1,0:T(8,128)(2,1)}, bf16[2,256,256]{2,1,0:T(8,128)(2,1)}, u32[]{:S(2)}, u32[]{:S(2)}) collective-permute-start(bf16[2,256,256]{2,1,0:T(8,128)(2,1)} %get-tuple-element.33), channel_id=1, source_target_pairs={{0,3},{1,0},{2,1},{3,2},{4,7},{5,4},{6,5},{7,6},{8,11},{9,8},{10,9... | collective-permute-start | bytes 786440 | tf_op jit(solution)/shard_map/ppermute | solution.py:339
  71.9 3.3 %roll_planes.1.refs_1_ = bf16[8,2,128,256]{3,2,1,0:T(8,128)(2,1)} custom-call(s32[2]{0:T(128)} %pad_add_fusion.place_ref, bf16[8,4,128,256]{3,2,1,0:T(8,128)(2,1)} %all-to-all-done.1.refs_1_.blocks_hbm.refs_0_, bf16[8,4,128,256]{3,2,1,0:T(8,128)(2,1)} %all-to-all-done.1.refs_1_.blocks_hbm.refs_0_), custom_call_target="tpu_custom_call" | custom-call | tf_op jit(solution)/shard_map/roll_planes/pallas_call | solution.py:255
  75.2 1.9 %all-to-all-done.2.refs_0_ = bf16[8,2,128,256]{3,2,1,0:T(8,128)(2,1)} async-done(((bf16[8,2,128,256]{3,2,1,0:T(8,128)(2,1)}), bf16[8,2,128,256]{3,2,1,0:T(8,128)(2,1)}, u32[]{:S(2)}, u32[]{:S(2)}) %all-to-all-start.2) | async-done | bytes 1048608 | tf_op jit(solution)/shard_map/all_to_all | solution.py:333
  77.1 5.7 %all-to-all-start.3 = ((bf16[8,2,128,256]{3,2,1,0:T(8,128)(2,1)}), bf16[8,2,128,256]{3,2,1,0:T(8,128)(2,1)}, u32[]{:S(2)}, u32[]{:S(2)}) async-start(bf16[8,2,128,256]{3,2,1,0:T(8,128)(2,1)} %roll_planes.1.refs_1_), calls=%async_computation.3 | async-start | bytes 2097152 | tf_op jit(solution)/shard_map/all_to_all | solution.py:333
  82.8 4.7 %y_transform.5 = (bf16[2,128,256]{2,1,0:T(8,128)(2,1)}, bf16[2,128,256]{2,1,0:T(8,128)(2,1)}, bf16[2,128,256]{2,1,0:T(8,128)(2,1)}, bf16[2,128,256]{2,1,0:T(8,12...) custom-call(s32[2]{0:T(128)} %pad_add_fusion.place_ref, ...), custom_call_target="tpu_custom_call" | custom-call | tf_op jit(solution)/shard_map/y_transform/pallas_call | solution.py:123
  89.9 1.4 %collective-permute-start.8 = (bf16[2,128,256]{2,1,0:T(8,128)(2,1)}, bf16[2,128,256]{2,1,0:T(8,128)(2,1)}, u32[]{:S(2)}, u32[]{:S(2)}) collective-permute-start(bf16[2,128,256]{2,1,0:T(8,128)(2,1)} %get-tuple-element.30), channel_id=1, source_target_pairs={{0,3},{1,0},{2,1},{3,2},{4,7},{5,4},{6,5},{7,6},{8,11},{9,8},{10,9... | collective-permute-start | bytes 393224 | tf_op jit(solution)/shard_map/ppermute | solution.py:339
  91.3 5.4 %all-to-all-done.3.from_hbm = bf16[8,2,128,256]{3,2,1,0:T(8,128)(2,1)} async-done(((bf16[8,2,128,256]{3,2,1,0:T(8,128)(2,1)}), bf16[8,2,128,256]{3,2,1,0:T(8,128)(2,1)}, u32[]{:S(2)}, u32[]{:S(2)}) %all-to-all-start.3) | async-done | bytes 1048608 | tf_op jit(solution)/shard_map/all_to_all | solution.py:333
  96.7 2.0 %by_part.1 = bf16[2,8,128,256]{3,2,1,0:T(8,128)(2,1)} custom-call(bf16[8,2,128,256]{3,2,1,0:T(8,128)(2,1)} %all-to-all-done.3.from_hbm), custom_call_target="tpu_custom_call" | custom-call | tf_op jit(solution)/shard_map/by_part/pallas_call | solution.py:286
  101.2 4.9 %z_transform.5.refs_5_ = bf16[3,2,1,256,1024]{4,3,2,1,0:T(8,128)(2,1)} custom-call(s32[2]{0:T(128)} %pad_add_fusion.place_ref, bf16[2,256,256]{2,1,0:T(8,128)(2,1)} %get-tuple-element.21.refs_1_.refs_0_, bf16[2,256,256]{2,1,0:T(8,128)(2,1)} %collective-permute-done.9.refs_1_, ...), custom_call_target="tpu_custom_call", output_to_operand_aliasing={{}: (6, {})} | custom-call | tf_op jit(solution)/shard_map/z_transform/pallas_call | solution.py:211
  106.2 1.4 %collective-permute-start.5 = (bf16[2,128,256]{2,1,0:T(8,128)(2,1)}, bf16[2,128,256]{2,1,0:T(8,128)(2,1)}, u32[]{:S(2)}, u32[]{:S(2)}) collective-permute-start(bf16[2,128,256]{2,1,0:T(8,128)(2,1)} %get-tuple-element.26), channel_id=1, source_target_pairs={{0,3},{1,0},{2,1},{3,2},{4,7},{5,4},{6,5},{7,6},{8,11},{9,8},{10,9... | collective-permute-start | bytes 393224 | tf_op jit(solution)/shard_map/ppermute | solution.py:339
  107.6 4.0 %z_transform.6.refs_5_ = bf16[3,2,1,256,1024]{4,3,2,1,0:T(8,128)(2,1)} custom-call(s32[2]{0:T(128)} %pad_add_fusion.place_ref, bf16[2,128,256]{2,1,0:T(8,128)(2,1)} %after.9.refs_0_, bf16[2,128,256]{2,1,0:T(8,128)(2,1)} %collective-permute-done.6.refs_1_, bf16[2,128,256]{2,1,0:T(8,128)(2,1)} %collective-permute-done.7.refs_2_, ...), custom_call_target="tpu_custom_call", output_to_operand_aliasing={{}: (6, {})} | custom-call | flops 40000000000 | tf_op jit(solution)/shard_map/z_transform/pallas_call | solution.py:211
  111.6 2.2 %collective-permute-done.5.refs_3_ = bf16[2,128,256]{2,1,0:T(8,128)(2,1)} collective-permute-done((bf16[2,128,256]{2,1,0:T(8,128)(2,1)}, bf16[2,128,256]{2,1,0:T(8,128)(2,1)}, u32[]{:S(2)}, u32[]{:S(2)}) %collective-permute-start.5) | collective-permute-done | bytes 131104 | tf_op jit(solution)/shard_map/ppermute | solution.py:339
  113.8 4.0 %z_transform.7 = bf16[3,2,1,256,1024]{4,3,2,1,0:T(8,128)(2,1)} custom-call(s32[2]{0:T(128)} %pad_add_fusion.place_ref, bf16[2,128,256]{2,1,0:T(8,128)(2,1)} %get-tuple-element.23.refs_0_, bf16[2,128,256]{2,1,0:T(8,128)(2,1)} %collective-permute-done.3.refs_1_, bf16[2,128,256]{2,1,0:T(8,128)(2,1)} %collective-permute-done.4.refs_2_, ...), custom_call_target="tpu_custom_call", output_to_operand_aliasing={{}: (6, {})} | custom-call | tf_op jit(solution)/shard_map/z_transform/pallas_call | solution.py:211
  (27 shorter events, 14.7 us)
Async XLA Ops:
  2.7 18.9 %all-to-all-start = ((bf16[8,2,128,256]{3,2,1,0:T(8,128)(2,1)}), bf16[8,2,128,256]{3,2,1,0:T(8,128)(2,1)}, u32[]{:S(2)}, u32[]{:S(2)}) async-start(bf16[8,2,128,256]{3,2,1,0:T(8,128)(2,1)} %by_plane.5), calls=%async_computation | async-start | bytes 2097152 | tf_op jit(solution)/shard_map/all_to_all | solution.py:333
  21.6 31.0 %all-to-all-start.1 = ((bf16[8,4,128,256]{3,2,1,0:T(8,128)(2,1)}), bf16[8,4,128,256]{3,2,1,0:T(8,128)(2,1)}, u32[]{:S(2)}, u32[]{:S(2)}) async-start(bf16[8,4,128,256]{3,2,1,0:T(8,128)(2,1)} %after.5), calls=%async_computation.1 | async-start | bytes 4194304 | tf_op jit(solution)/shard_map/all_to_all | solution.py:333
  32.1 25.2 %collective-permute-start = (bf16[2,256,256]{2,1,0:T(8,128)(2,1)}, bf16[2,256,256]{2,1,0:T(8,128)(2,1)}, u32[]{:S(2)}, u32[]{:S(2)}) collective-permute-start(bf16[2,256,256]{2,1,0:T(8,128)(2,1)} %get-tuple-element.18), channel_id=1, source_target_pairs={{0,1},{1,2},{2,3},{3,0},{4,5},{5,6},{6,7},{7,4},{8,9},{9,10},{10,1... | collective-permute-start | bytes 786440 | tf_op jit(solution)/shard_map/ppermute | solution.py:339
  33.4 23.9 %collective-permute-start.1 = (bf16[2,256,256]{2,1,0:T(8,128)(2,1)}, bf16[2,256,256]{2,1,0:T(8,128)(2,1)}, u32[]{:S(2)}, u32[]{:S(2)}) collective-permute-start(bf16[2,256,256]{2,1,0:T(8,128)(2,1)} %get-tuple-element.19), channel_id=1, source_target_pairs={{0,2},{1,3},{2,0},{3,1},{4,6},{5,7},{6,4},{7,5},{8,10},{9,11},{10,... | collective-permute-start | bytes 786440 | tf_op jit(solution)/shard_map/ppermute | solution.py:339
  34.5 23.9 %collective-permute-start.2 = (bf16[2,256,256]{2,1,0:T(8,128)(2,1)}, bf16[2,256,256]{2,1,0:T(8,128)(2,1)}, u32[]{:S(2)}, u32[]{:S(2)}) collective-permute-start(bf16[2,256,256]{2,1,0:T(8,128)(2,1)} %get-tuple-element.20), channel_id=1, source_target_pairs={{0,3},{1,0},{2,1},{3,2},{4,7},{5,4},{6,5},{7,6},{8,11},{9,8},{10,9... | collective-permute-start | bytes 786440 | tf_op jit(solution)/shard_map/ppermute | solution.py:339
  58.4 18.6 %all-to-all-start.2 = ((bf16[8,2,128,256]{3,2,1,0:T(8,128)(2,1)}), bf16[8,2,128,256]{3,2,1,0:T(8,128)(2,1)}, u32[]{:S(2)}, u32[]{:S(2)}) async-start(bf16[8,2,128,256]{3,2,1,0:T(8,128)(2,1)} %after.7), calls=%async_computation.2 | async-start | bytes 2097152 | tf_op jit(solution)/shard_map/all_to_all | solution.py:333
  63.1 26.8 %collective-permute-start.9 = (bf16[2,256,256]{2,1,0:T(8,128)(2,1)}, bf16[2,256,256]{2,1,0:T(8,128)(2,1)}, u32[]{:S(2)}, u32[]{:S(2)}) collective-permute-start(bf16[2,256,256]{2,1,0:T(8,128)(2,1)} %get-tuple-element.31), channel_id=1, source_target_pairs={{0,1},{1,2},{2,3},{3,0},{4,5},{5,6},{6,7},{7,4},{8,9},{9,10},{10,1... | collective-permute-start | bytes 786440 | tf_op jit(solution)/shard_map/ppermute | solution.py:339
  69.3 29.4 %collective-permute-start.10 = (bf16[2,256,256]{2,1,0:T(8,128)(2,1)}, bf16[2,256,256]{2,1,0:T(8,128)(2,1)}, u32[]{:S(2)}, u32[]{:S(2)}) collective-permute-start(bf16[2,256,256]{2,1,0:T(8,128)(2,1)} %get-tuple-element.32), channel_id=1, source_target_pairs={{0,2},{1,3},{2,0},{3,1},{4,6},{5,7},{6,4},{7,5},{8,10},{9,11},{10,... | collective-permute-start | bytes 786440 | tf_op jit(solution)/shard_map/ppermute | solution.py:339
  70.4 29.7 %collective-permute-start.11 = (bf16[2,256,256]{2,1,0:T(8,128)(2,1)}, bf16[2,256,256]{2,1,0:T(8,128)(2,1)}, u32[]{:S(2)}, u32[]{:S(2)}) collective-permute-start(bf16[2,256,256]{2,1,0:T(8,128)(2,1)} %get-tuple-element.33), channel_id=1, source_target_pairs={{0,3},{1,0},{2,1},{3,2},{4,7},{5,4},{6,5},{7,6},{8,11},{9,8},{10,9... | collective-permute-start | bytes 786440 | tf_op jit(solution)/shard_map/ppermute | solution.py:339
  77.1 19.7 %all-to-all-start.3 = ((bf16[8,2,128,256]{3,2,1,0:T(8,128)(2,1)}), bf16[8,2,128,256]{3,2,1,0:T(8,128)(2,1)}, u32[]{:S(2)}, u32[]{:S(2)}) async-start(bf16[8,2,128,256]{3,2,1,0:T(8,128)(2,1)} %roll_planes.1.refs_1_), calls=%async_computation.3 | async-start | bytes 2097152 | tf_op jit(solution)/shard_map/all_to_all | solution.py:333
  87.5 18.7 %collective-permute-start.6 = (bf16[2,128,256]{2,1,0:T(8,128)(2,1)}, bf16[2,128,256]{2,1,0:T(8,128)(2,1)}, u32[]{:S(2)}, u32[]{:S(2)}) collective-permute-start(bf16[2,128,256]{2,1,0:T(8,128)(2,1)} %get-tuple-element.28), channel_id=1, source_target_pairs={{0,1},{1,2},{2,3},{3,0},{4,5},{5,6},{6,7},{7,4},{8,9},{9,10},{10,1... | collective-permute-start | bytes 393224 | tf_op jit(solution)/shard_map/ppermute | solution.py:339
  88.8 18.8 %collective-permute-start.7 = (bf16[2,128,256]{2,1,0:T(8,128)(2,1)}, bf16[2,128,256]{2,1,0:T(8,128)(2,1)}, u32[]{:S(2)}, u32[]{:S(2)}) collective-permute-start(bf16[2,128,256]{2,1,0:T(8,128)(2,1)} %get-tuple-element.29), channel_id=1, source_target_pairs={{0,2},{1,3},{2,0},{3,1},{4,6},{5,7},{6,4},{7,5},{8,10},{9,11},{10,... | collective-permute-start | bytes 393224 | tf_op jit(solution)/shard_map/ppermute | solution.py:339
  89.9 17.7 %collective-permute-start.8 = (bf16[2,128,256]{2,1,0:T(8,128)(2,1)}, bf16[2,128,256]{2,1,0:T(8,128)(2,1)}, u32[]{:S(2)}, u32[]{:S(2)}) collective-permute-start(bf16[2,128,256]{2,1,0:T(8,128)(2,1)} %get-tuple-element.30), channel_id=1, source_target_pairs={{0,3},{1,0},{2,1},{3,2},{4,7},{5,4},{6,5},{7,6},{8,11},{9,8},{10,9... | collective-permute-start | bytes 393224 | tf_op jit(solution)/shard_map/ppermute | solution.py:339
  98.8 12.8 %collective-permute-start.3 = (bf16[2,128,256]{2,1,0:T(8,128)(2,1)}, bf16[2,128,256]{2,1,0:T(8,128)(2,1)}, u32[]{:S(2)}, u32[]{:S(2)}) collective-permute-start(bf16[2,128,256]{2,1,0:T(8,128)(2,1)} %get-tuple-element.24), channel_id=1, source_target_pairs={{0,1},{1,2},{2,3},{3,0},{4,5},{5,6},{6,7},{7,4},{8,9},{9,10},{10,1... | collective-permute-start | bytes 393224 | tf_op jit(solution)/shard_map/ppermute | solution.py:339
  100.1 11.5 %collective-permute-start.4 = (bf16[2,128,256]{2,1,0:T(8,128)(2,1)}, bf16[2,128,256]{2,1,0:T(8,128)(2,1)}, u32[]{:S(2)}, u32[]{:S(2)}) collective-permute-start(bf16[2,128,256]{2,1,0:T(8,128)(2,1)} %get-tuple-element.25), channel_id=1, source_target_pairs={{0,2},{1,3},{2,0},{3,1},{4,6},{5,7},{6,4},{7,5},{8,10},{9,11},{10,... | collective-permute-start | bytes 393224 | tf_op jit(solution)/shard_map/ppermute | solution.py:339
  106.2 7.7 %collective-permute-start.5 = (bf16[2,128,256]{2,1,0:T(8,128)(2,1)}, bf16[2,128,256]{2,1,0:T(8,128)(2,1)}, u32[]{:S(2)}, u32[]{:S(2)}) collective-permute-start(bf16[2,128,256]{2,1,0:T(8,128)(2,1)} %get-tuple-element.26), channel_id=1, source_target_pairs={{0,3},{1,0},{2,1},{3,2},{4,7},{5,4},{6,5},{7,6},{8,11},{9,8},{10,9... | collective-permute-start | bytes 393224 | tf_op jit(solution)/shard_map/ppermute | solution.py:339
where the time goes:
time: 120 us; the launch traced here: 118 us
  Pallas kernels  43.7 us (36%)
  starting transfers between devices  36.6 us (30%)
  waiting for transfers between devices  34.3 us (29%)
  local copies, waits for them, and re-layouts  1.31 us (1%)
  other arithmetic  1.2 us (1%)
    all_to_all x4, waiting for transfers between devices, exchange(): return lax.all_to_all(blocks, 'ky', 0, 0, tiled=True)  30.9 us
    all_to_all x4, starting transfers between devices, exchange(): return lax.all_to_all(blocks, 'ky', 0, 0, tiled=True)  21.2 us
    pallas_call x4, Pallas kernels, z_transform(): pl.pallas_call(functools.partial(z_kernel, layout, targets, component, fi...  17.8 us
    ppermute x12, starting transfers between devices, along_z(): lax.ppermute(piece, 'kz', [(i, (i + step) % targets) for i in range(targe...  15.3 us
    pallas_call x3, Pallas kernels, y_transform(): pl.pallas_call(functools.partial(y_kernel, targets, halves), out_shape=[j...  14 us
    pallas_call x4, Pallas kernels, restack(): pl.pallas_call(functools.partial(restack_kernel, steps), out_shape=jax.Sh...  8.54 us
    ppermute x12, waiting for transfers between devices, along_z(): lax.ppermute(piece, 'kz', [(i, (i + step) % targets) for i in range(targe...  3.38 us
    pallas_call x1, Pallas kernels, roll_planes(): pl.pallas_call(functools.partial(roll_kernel, [number for _, number in sl...  3.33 us
  transfers between devices with their start and end apart: 16, of which 6 were waited for; matrix products, arithmetic and copies ran while one was open for 2% of the time, Pallas kernels for 32%

commit v1 on v0

--- a/solution.py
+++ b/solution.py
@@ -12,6 +12,7 @@
 
 VMEM_LIMIT = 64 * 1024 * 1024
 COST = pl.CostEstimate(flops=0, bytes_accessed=0, transcendentals=0)
+MID = pl.CostEstimate(flops=8_000_000_000, bytes_accessed=0, transcendentals=0)
 HIGH = pl.CostEstimate(flops=40_000_000_000, bytes_accessed=0, transcendentals=0)
 
 
@@ -282,14 +283,14 @@
         copy.wait()
 
 
-def restack(array, steps, shape, name):
+def restack(array, steps, part, shape, name):
     return pl.pallas_call(
         functools.partial(restack_kernel, steps),
         out_shape=jax.ShapeDtypeStruct(shape, array.dtype),
         in_specs=[IN_HBM],
         out_specs=IN_HBM,
         scratch_shapes=[
-            pltpu.VMEM((len(steps), array.shape[-3] if array.ndim == 5 else array.shape[0], *array.shape[-2:]), array.dtype),
+            pltpu.VMEM((len(steps), *part), array.dtype),
             pltpu.SemaphoreType.DMA((len(steps),)),
             pltpu.SemaphoreType.DMA((len(steps),)),
         ],
@@ -299,16 +300,21 @@
     )(array)
 
 
-def by_plane(fields, *slots):
+def by_plane(fields, *slots, lanes=None):
     _, _, planes, rows, columns = fields.shape
-    steps = [(slot, (slice(None), number)) for number, slot in enumerate(slots)]
-    return restack(fields, steps, (planes, len(slots), rows, columns), "by_plane")
+    start, stop = lanes or (0, columns)
+    steps = [
+        ((*slot, slice(None), slice(None), pl.ds(start, stop - start)), (slice(None), number))
+        for number, slot in enumerate(slots)
+    ]
+    part = (planes, rows, stop - start)
+    return restack(fields, steps, part, (planes, len(slots), rows, stop - start), "by_plane")
 
 
 def by_part(planes):
     count, parts, rows, columns = planes.shape
     steps = [((slice(None), part), (part,)) for part in range(parts)]
-    return restack(planes, steps, (parts, count, rows, columns), "by_part")
+    return restack(planes, steps, (count, rows, columns), (parts, count, rows, columns), "by_part")
 
 
 def nothing_kernel(*refs):
@@ -362,20 +368,21 @@
         return z_transform(pieces, layout, place, kz_table, targets, component, first_row, field, shape, cost)
 
     by_rows = [(0, 0), (y_rows // 2, 0)]
-    blocks0 = exchange(by_plane(fields, (0, 0), (0, 1)))
-    blocks1 = exchange(after(by_plane(fields, (1, 0), (1, 1), (components, 0), (components, 1)), blocks0))
-    pieces0 = y_of(blocks0, 1, HIGH)[0]
-    pieces1 = y_of(blocks1, 1)[0]
-    third = after(by_plane(fields, (2, 0), (2, 1)), blocks1, *pieces0[1:])
-    blocks2 = exchange(after(third, pieces1[0], cost=HIGH))
+    fields0 = by_plane(fields, (0, 0), (0, 1))
+    fields1 = by_plane(fields, (1, 0), (1, 1))
+    fields2 = by_plane(fields, (2, 0), (2, 1), (components, 0), (components, 1))
+    blocks0 = exchange(fields0)
+    (pieces0,) = y_of(blocks0, 1, HIGH)
+    blocks1 = exchange(fields1)
+    (pieces1,) = y_of(blocks1, 1, MID)
+    blocks2 = exchange(fields2)
     field = z_of([pieces0], by_rows[:1], 0, 0, None, HIGH)
-    pieces2, pieces3 = y_of(after(blocks2, field), 2)
-    plane = roll_planes(place, (blocks1, 2), (blocks1, 3))
+    blocks2 = after(blocks2, field)
+    (pieces2,) = y_of(blocks2, 1)
+    plane = roll_planes(place, (blocks2, 2), (blocks2, 3))
     scalar = by_part(exchange(plane))
     field = z_of([pieces1], by_rows[:1], 1, 0, field)
-    pieces2[0] = after(pieces2[0], plane, cost=HIGH)
     field = z_of([pieces2], by_rows[:1], 2, 0, field, HIGH)
-    field = z_of([pieces3], by_rows[:1], 2, y_rows // 2, field)
     return (field, scalar)
 
 

time: 120 us -> 111 us (0.925); the launches traced: 118 us -> 110 us
  starting transfers between devices: 36.6 us -> 32.4 us
  Pallas kernels: 43.7 us -> 40.6 us
    all_to_all x4, waiting for transfers between devices: 30.9 us -> 12.3 us  [exchange(): return lax.all_to_all(blocks, 'ky', 0, 0, tiled=True)]
    ppermute x12 -> x9, waiting for transfers between devices: 3.38 us -> 21.7 us  [along_z(): lax.ppermute(piece, 'kz', [(i, (i + step) % targets) for i in range(targe...]
    ppermute x12 -> x9, starting transfers between devices: 15.3 us -> 9.27 us  [along_z(): lax.ppermute(piece, 'kz', [(i, (i + step) % targets) for i in range(targe...]
    pallas_call x4 -> x3, Pallas kernels: 17.8 us -> 14.8 us  [z_transform(): pl.pallas_call(functools.partial(z_kernel, layout, targets, component, fi...]
    all_to_all x4, starting transfers between devices: 21.2 us -> 23.1 us  [exchange(): return lax.all_to_all(blocks, 'ky', 0, 0, tiled=True)]
  transfers between devices with their start and end apart: 16 -> 13, of which waited for: 6 -> 6; matrix products, arithmetic and copies ran while one was open for 2% -> 2% of each run, Pallas kernels for 32% -> 33%
where the time goes in v1:
time: 111 us; the launch traced here: 110 us
  Pallas kernels  40.6 us (37%)
  waiting for transfers between devices  34 us (31%)
  starting transfers between devices  32.4 us (29%)
  local copies, waits for them, and re-layouts  1.32 us (1%)
  other arithmetic  1.28 us (1%)
    all_to_all x4, starting transfers between devices, exchange(): return lax.all_to_all(blocks, 'ky', 0, 0, tiled=True)  23.1 us
    ppermute x9, waiting for transfers between devices, along_z(): lax.ppermute(piece, 'kz', [(i, (i + step) % targets) for i in range(targe...  21.7 us
    pallas_call x3, Pallas kernels, z_transform(): pl.pallas_call(functools.partial(z_kernel, layout, targets, component, fi...  14.8 us
    pallas_call x3, Pallas kernels, y_transform(): pl.pallas_call(functools.partial(y_kernel, targets, halves), out_shape=[j...  13.9 us
    all_to_all x4, waiting for transfers between devices, exchange(): return lax.all_to_all(blocks, 'ky', 0, 0, tiled=True)  12.3 us
    ppermute x9, starting transfers between devices, along_z(): lax.ppermute(piece, 'kz', [(i, (i + step) % targets) for i in range(targe...  9.27 us
    pallas_call x4, Pallas kernels, restack(): pl.pallas_call(functools.partial(restack_kernel, steps), out_shape=jax.Sh...  8.58 us
    pallas_call x1, Pallas kernels, roll_planes(): pl.pallas_call(functools.partial(roll_kernel, [number for _, number in sl...  3.31 us
  transfers between devices with their start and end apart: 13, of which 6 were waited for; matrix products, arithmetic and copies ran while one was open for 2% of the time, Pallas kernels for 33%

profile of v1, /device:TPU:11, one launch (start us, length us, event | category | flops | bytes accessed | tf_op | source)
XLA Modules:
  0.0 110.4 jit_solution(9654385055461063064)
XLA Ops:
  0.6 2.0 %by_plane.4 = bf16[8,2,128,256]{3,2,1,0:T(8,128)(2,1)} custom-call(bf16[4,2,8,128,256]{4,3,2,1,0:T(8,128)(2,1)} %from_hbm.5), custom_call_target="tpu_custom_call" | custom-call | tf_op jit(solution)/shard_map/by_plane/pallas_call | solution.py:287
  2.7 5.0 %all-to-all-start.1 = ((bf16[8,2,128,256]{3,2,1,0:T(8,128)(2,1)}), bf16[8,2,128,256]{3,2,1,0:T(8,128)(2,1)}, u32[]{:S(2)}, u32[]{:S(2)}) async-start(bf16[8,2,128,256]{3,2,1,0:T(8,128)(2,1)} %by_plane.4), calls=%async_computation.1 | async-start | bytes 2097152 | tf_op jit(solution)/shard_map/all_to_all | solution.py:339
  7.7 2.0 %by_plane.5 = bf16[8,2,128,256]{3,2,1,0:T(8,128)(2,1)} custom-call(bf16[4,2,8,128,256]{4,3,2,1,0:T(8,128)(2,1)} %from_hbm.5), custom_call_target="tpu_custom_call" | custom-call | tf_op jit(solution)/shard_map/by_plane/pallas_call | solution.py:287
  9.7 2.5 %by_plane.3 = bf16[8,4,128,256]{3,2,1,0:T(8,128)(2,1)} custom-call(bf16[4,2,8,128,256]{4,3,2,1,0:T(8,128)(2,1)} %from_hbm.5), custom_call_target="tpu_custom_call" | custom-call | tf_op jit(solution)/shard_map/by_plane/pallas_call | solution.py:287
  14.8 6.8 %all-to-all-done.1.blocks_hbm = bf16[8,2,128,256]{3,2,1,0:T(8,128)(2,1)} async-done(((bf16[8,2,128,256]{3,2,1,0:T(8,128)(2,1)}), bf16[8,2,128,256]{3,2,1,0:T(8,128)(2,1)}, u32[]{:S(2)}, u32[]{:S(2)}) %all-to-all-start.1) | async-done | bytes 1048608 | tf_op jit(solution)/shard_map/all_to_all | solution.py:339
  21.6 5.7 %all-to-all-start.2 = ((bf16[8,2,128,256]{3,2,1,0:T(8,128)(2,1)}), bf16[8,2,128,256]{3,2,1,0:T(8,128)(2,1)}, u32[]{:S(2)}, u32[]{:S(2)}) async-start(bf16[8,2,128,256]{3,2,1,0:T(8,128)(2,1)} %by_plane.5), calls=%async_computation.2 | async-start | bytes 2097152 | tf_op jit(solution)/shard_map/all_to_all | solution.py:339
  27.3 4.6 %y_transform.3 = (bf16[2,256,256]{2,1,0:T(8,128)(2,1)}, bf16[2,256,256]{2,1,0:T(8,128)(2,1)}, bf16[2,256,256]{2,1,0:T(8,128)(2,1)}, bf16[2,256,256]{2,1,0:T(8,128)(2,1)}) custom-call(s32[2]{0:T(128)} %pad_add_fusion.place_ref, bf16[8,2,128,256]{3,2,1,0:T(8,128)(2,1)} %all-to-all-done.1.blocks_hbm, bf16[2,512,1024]{2,1,0:T(8,128)(2,1)} %constant.17.clone.table_hbm), custom_call_target="tpu_custom_call" | custom-call | flops 40000000000 | tf_op jit(solution)/shard_map/y_transform/pallas_call | solution.py:124
  34.4 1.4 %collective-permute-start.2 = (bf16[2,256,256]{2,1,0:T(8,128)(2,1)}, bf16[2,256,256]{2,1,0:T(8,128)(2,1)}, u32[]{:S(2)}, u32[]{:S(2)}) collective-permute-start(bf16[2,256,256]{2,1,0:T(8,128)(2,1)} %get-tuple-element.17), channel_id=1, source_target_pairs={{0,3},{1,0},{2,1},{3,2},{4,7},{5,4},{6,5},{7,6},{8,11},{9,8},{10,9... | collective-permute-start | bytes 786440 | tf_op jit(solution)/shard_map/ppermute | solution.py:345
  35.8 5.4 %all-to-all-done.2.blocks_hbm = bf16[8,2,128,256]{3,2,1,0:T(8,128)(2,1)} async-done(((bf16[8,2,128,256]{3,2,1,0:T(8,128)(2,1)}), bf16[8,2,128,256]{3,2,1,0:T(8,128)(2,1)}, u32[]{:S(2)}, u32[]{:S(2)}) %all-to-all-start.2) | async-done | bytes 1048608 | tf_op jit(solution)/shard_map/all_to_all | solution.py:339
  41.3 5.8 %all-to-all-start = ((bf16[8,4,128,256]{3,2,1,0:T(8,128)(2,1)}), bf16[8,4,128,256]{3,2,1,0:T(8,128)(2,1)}, u32[]{:S(2)}, u32[]{:S(2)}) async-start(bf16[8,4,128,256]{3,2,1,0:T(8,128)(2,1)} %by_plane.3), calls=%async_computation | async-start | bytes 4194304 | tf_op jit(solution)/shard_map/all_to_all | solution.py:339
  47.1 4.6 %y_transform.5 = (bf16[2,256,256]{2,1,0:T(8,128)(2,1)}, bf16[2,256,256]{2,1,0:T(8,128)(2,1)}, bf16[2,256,256]{2,1,0:T(8,128)(2,1)}, bf16[2,256,256]{2,1,0:T(8,128)(2,1)}) custom-call(s32[2]{0:T(128)} %pad_add_fusion.place_ref, bf16[8,2,128,256]{3,2,1,0:T(8,128)(2,1)} %all-to-all-done.2.blocks_hbm, bf16[2,512,1024]{2,1,0:T(8,128)(2,1)} %constant.17.clone.table_hbm), custom_call_target="tpu_custom_call" | custom-call | flops 8000000000 | tf_op jit(solution)/shard_map/y_transform/pallas_call | solution.py:124
  51.8 1.4 %collective-permute-start.6 = (bf16[2,256,256]{2,1,0:T(8,128)(2,1)}, bf16[2,256,256]{2,1,0:T(8,128)(2,1)}, u32[]{:S(2)}, u32[]{:S(2)}) collective-permute-start(bf16[2,256,256]{2,1,0:T(8,128)(2,1)} %get-tuple-element.23), channel_id=1, source_target_pairs={{0,1},{1,2},{2,3},{3,0},{4,5},{5,6},{6,7},{7,4},{8,9},{9,10},{10,1... | collective-permute-start | bytes 786440 | tf_op jit(solution)/shard_map/ppermute | solution.py:345
  54.2 1.4 %collective-permute-start.8 = (bf16[2,256,256]{2,1,0:T(8,128)(2,1)}, bf16[2,256,256]{2,1,0:T(8,128)(2,1)}, u32[]{:S(2)}, u32[]{:S(2)}) collective-permute-start(bf16[2,256,256]{2,1,0:T(8,128)(2,1)} %get-tuple-element.25), channel_id=1, source_target_pairs={{0,3},{1,0},{2,1},{3,2},{4,7},{5,4},{6,5},{7,6},{8,11},{9,8},{10,9... | collective-permute-start | bytes 786440 | tf_op jit(solution)/shard_map/ppermute | solution.py:345
  55.8 13.8 %collective-permute-done.2.refs_3_ = bf16[2,256,256]{2,1,0:T(8,128)(2,1)} collective-permute-done((bf16[2,256,256]{2,1,0:T(8,128)(2,1)}, bf16[2,256,256]{2,1,0:T(8,128)(2,1)}, u32[]{:S(2)}, u32[]{:S(2)}) %collective-permute-start.2) | collective-permute-done | bytes 262176 | tf_op jit(solution)/shard_map/ppermute | solution.py:345
  69.6 4.9 %z_transform.3.refs_1_.refs_5_ = bf16[3,2,1,256,1024]{4,3,2,1,0:T(8,128)(2,1)} custom-call(s32[2]{0:T(128)} %pad_add_fusion.place_ref, bf16[2,256,256]{2,1,0:T(8,128)(2,1)} %get-tuple-element.14.refs_0_, bf16[2,256,256]{2,1,0:T(8,128)(2,1)} %collective-permute-done.refs_1_, bf16[2,256,256]{2,1,0:T(8,128)(2,1)} %collective-permute-done.1.refs_2_, ...), custom_call_target="tpu_custom_call" | custom-call | flops 40000000000 | tf_op jit(solution)/shard_map/z_transform/pallas_call | solution.py:212
  74.5 4.7 %y_transform.4 = (bf16[2,256,256]{2,1,0:T(8,128)(2,1)}, bf16[2,256,256]{2,1,0:T(8,128)(2,1)}, bf16[2,256,256]{2,1,0:T(8,128)(2,1)}, bf16[2,256,256]{2,1,0:T(8,128)(2,1)}) custom-call(s32[2]{0:T(128)} %pad_add_fusion.place_ref, bf16[8,4,128,256]{3,2,1,0:T(8,128)(2,1)} %after.1.blocks_hbm.refs_0_.refs_1_, bf16[2,512,1024]{2,1,0:T(8,128)(2,1)} %constant.17.clone.table_hbm), custom_call_target="tpu_custom_call" | custom-call | tf_op jit(solution)/shard_map/y_transform/pallas_call | solution.py:124
  79.4 1.4 %collective-permute-start.5 = (bf16[2,256,256]{2,1,0:T(8,128)(2,1)}, bf16[2,256,256]{2,1,0:T(8,128)(2,1)}, u32[]{:S(2)}, u32[]{:S(2)}) collective-permute-start(bf16[2,256,256]{2,1,0:T(8,128)(2,1)} %get-tuple-element.21), channel_id=1, source_target_pairs={{0,3},{1,0},{2,1},{3,2},{4,7},{5,4},{6,5},{7,6},{8,11},{9,8},{10,9... | collective-permute-start | bytes 786440 | tf_op jit(solution)/shard_map/ppermute | solution.py:345
  80.8 3.3 %roll_planes.1 = bf16[8,2,128,256]{3,2,1,0:T(8,128)(2,1)} custom-call(s32[2]{0:T(128)} %pad_add_fusion.place_ref, bf16[8,4,128,256]{3,2,1,0:T(8,128)(2,1)} %after.1.blocks_hbm.refs_0_.refs_1_, bf16[8,4,128,256]{3,2,1,0:T(8,128)(2,1)} %after.1.blocks_hbm.refs_0_.refs_1_), custom_call_target="tpu_custom_call" | custom-call | tf_op jit(solution)/shard_map/roll_planes/pallas_call | solution.py:256
  84.1 6.6 %all-to-all-start.3 = ((bf16[8,2,128,256]{3,2,1,0:T(8,128)(2,1)}), bf16[8,2,128,256]{3,2,1,0:T(8,128)(2,1)}, u32[]{:S(2)}, u32[]{:S(2)}) async-start(bf16[8,2,128,256]{3,2,1,0:T(8,128)(2,1)} %roll_planes.1), calls=%async_computation.3 | async-start | bytes 2097152 | tf_op jit(solution)/shard_map/all_to_all | solution.py:339
  90.7 4.9 %z_transform.4.refs_5_ = bf16[3,2,1,256,1024]{4,3,2,1,0:T(8,128)(2,1)} custom-call(s32[2]{0:T(128)} %pad_add_fusion.place_ref, bf16[2,256,256]{2,1,0:T(8,128)(2,1)} %get-tuple-element.22.refs_0_, bf16[2,256,256]{2,1,0:T(8,128)(2,1)} %collective-permute-done.6.refs_1_, ...), custom_call_target="tpu_custom_call", output_to_operand_aliasing={{}: (6, {})} | custom-call | tf_op jit(solution)/shard_map/z_transform/pallas_call | solution.py:212
  95.6 6.2 %collective-permute-done.4.refs_2_ = bf16[2,256,256]{2,1,0:T(8,128)(2,1)} collective-permute-done((bf16[2,256,256]{2,1,0:T(8,128)(2,1)}, bf16[2,256,256]{2,1,0:T(8,128)(2,1)}, u32[]{:S(2)}, u32[]{:S(2)}) %collective-permute-start.4) | collective-permute-done | bytes 262176 | tf_op jit(solution)/shard_map/ppermute | solution.py:345
  101.8 1.6 %collective-permute-done.5.refs_3_ = bf16[2,256,256]{2,1,0:T(8,128)(2,1)} collective-permute-done((bf16[2,256,256]{2,1,0:T(8,128)(2,1)}, bf16[2,256,256]{2,1,0:T(8,128)(2,1)}, u32[]{:S(2)}, u32[]{:S(2)}) %collective-permute-start.5) | collective-permute-done | bytes 262176 | tf_op jit(solution)/shard_map/ppermute | solution.py:345
  103.4 4.9 %z_transform.5 = bf16[3,2,1,256,1024]{4,3,2,1,0:T(8,128)(2,1)} custom-call(s32[2]{0:T(128)} %pad_add_fusion.place_ref, bf16[2,256,256]{2,1,0:T(8,128)(2,1)} %get-tuple-element.18.refs_0_, bf16[2,256,256]{2,1,0:T(8,128)(2,1)} %collective-permute-done.3.refs_1_, bf16[2,256,256]{2,1,0:T(8,128)(2,1)} %collective-permute-done.4.refs_2_, ...), custom_call_target="tpu_custom_call", output_to_operand_aliasing={{}: (6, {})} | custom-call | flops 40000000000 | tf_op jit(solution)/shard_map/z_transform/pallas_call | solution.py:212
  108.3 2.0 %by_part.1 = bf16[2,8,128,256]{3,2,1,0:T(8,128)(2,1)} custom-call(bf16[8,2,128,256]{3,2,1,0:T(8,128)(2,1)} %all-to-all-done.3.from_hbm), custom_call_target="tpu_custom_call" | custom-call | tf_op jit(solution)/shard_map/by_part/pallas_call | solution.py:287
  (16 shorter events, 6.6 us)
Async XLA Ops:
  2.7 18.9 %all-to-all-start.1 = ((bf16[8,2,128,256]{3,2,1,0:T(8,128)(2,1)}), bf16[8,2,128,256]{3,2,1,0:T(8,128)(2,1)}, u32[]{:S(2)}, u32[]{:S(2)}) async-start(bf16[8,2,128,256]{3,2,1,0:T(8,128)(2,1)} %by_plane.4), calls=%async_computation.1 | async-start | bytes 2097152 | tf_op jit(solution)/shard_map/all_to_all | solution.py:339
  21.6 19.7 %all-to-all-start.2 = ((bf16[8,2,128,256]{3,2,1,0:T(8,128)(2,1)}), bf16[8,2,128,256]{3,2,1,0:T(8,128)(2,1)}, u32[]{:S(2)}, u32[]{:S(2)}) async-start(bf16[8,2,128,256]{3,2,1,0:T(8,128)(2,1)} %by_plane.5), calls=%async_computation.2 | async-start | bytes 2097152 | tf_op jit(solution)/shard_map/all_to_all | solution.py:339
  32.0 22.2 %collective-permute-start = (bf16[2,256,256]{2,1,0:T(8,128)(2,1)}, bf16[2,256,256]{2,1,0:T(8,128)(2,1)}, u32[]{:S(2)}, u32[]{:S(2)}) collective-permute-start(bf16[2,256,256]{2,1,0:T(8,128)(2,1)} %get-tuple-element.15), channel_id=1, source_target_pairs={{0,1},{1,2},{2,3},{3,0},{4,5},{5,6},{6,7},{7,4},{8,9},{9,10},{10,1... | collective-permute-start | bytes 786440 | tf_op jit(solution)/shard_map/ppermute | solution.py:345
  33.3 22.5 %collective-permute-start.1 = (bf16[2,256,256]{2,1,0:T(8,128)(2,1)}, bf16[2,256,256]{2,1,0:T(8,128)(2,1)}, u32[]{:S(2)}, u32[]{:S(2)}) collective-permute-start(bf16[2,256,256]{2,1,0:T(8,128)(2,1)} %get-tuple-element.16), channel_id=1, source_target_pairs={{0,2},{1,3},{2,0},{3,1},{4,6},{5,7},{6,4},{7,5},{8,10},{9,11},{10,... | collective-permute-start | bytes 786440 | tf_op jit(solution)/shard_map/ppermute | solution.py:345
  34.4 35.1 %collective-permute-start.2 = (bf16[2,256,256]{2,1,0:T(8,128)(2,1)}, bf16[2,256,256]{2,1,0:T(8,128)(2,1)}, u32[]{:S(2)}, u32[]{:S(2)}) collective-permute-start(bf16[2,256,256]{2,1,0:T(8,128)(2,1)} %get-tuple-element.17), channel_id=1, source_target_pairs={{0,3},{1,0},{2,1},{3,2},{4,7},{5,4},{6,5},{7,6},{8,11},{9,8},{10,9... | collective-permute-start | bytes 786440 | tf_op jit(solution)/shard_map/ppermute | solution.py:345
  41.3 33.2 %all-to-all-start = ((bf16[8,4,128,256]{3,2,1,0:T(8,128)(2,1)}), bf16[8,4,128,256]{3,2,1,0:T(8,128)(2,1)}, u32[]{:S(2)}, u32[]{:S(2)}) async-start(bf16[8,4,128,256]{3,2,1,0:T(8,128)(2,1)} %by_plane.3), calls=%async_computation | async-start | bytes 4194304 | tf_op jit(solution)/shard_map/all_to_all | solution.py:339
  51.8 27.6 %collective-permute-start.6 = (bf16[2,256,256]{2,1,0:T(8,128)(2,1)}, bf16[2,256,256]{2,1,0:T(8,128)(2,1)}, u32[]{:S(2)}, u32[]{:S(2)}) collective-permute-start(bf16[2,256,256]{2,1,0:T(8,128)(2,1)} %get-tuple-element.23), channel_id=1, source_target_pairs={{0,1},{1,2},{2,3},{3,0},{4,5},{5,6},{6,7},{7,4},{8,9},{9,10},{10,1... | collective-permute-start | bytes 786440 | tf_op jit(solution)/shard_map/ppermute | solution.py:345
  53.1 37.6 %collective-permute-start.7 = (bf16[2,256,256]{2,1,0:T(8,128)(2,1)}, bf16[2,256,256]{2,1,0:T(8,128)(2,1)}, u32[]{:S(2)}, u32[]{:S(2)}) collective-permute-start(bf16[2,256,256]{2,1,0:T(8,128)(2,1)} %get-tuple-element.24), channel_id=1, source_target_pairs={{0,2},{1,3},{2,0},{3,1},{4,6},{5,7},{6,4},{7,5},{8,10},{9,11},{10,... | collective-permute-start | bytes 786440 | tf_op jit(solution)/shard_map/ppermute | solution.py:345
  54.2 36.5 %collective-permute-start.8 = (bf16[2,256,256]{2,1,0:T(8,128)(2,1)}, bf16[2,256,256]{2,1,0:T(8,128)(2,1)}, u32[]{:S(2)}, u32[]{:S(2)}) collective-permute-start(bf16[2,256,256]{2,1,0:T(8,128)(2,1)} %get-tuple-element.25), channel_id=1, source_target_pairs={{0,3},{1,0},{2,1},{3,2},{4,7},{5,4},{6,5},{7,6},{8,11},{9,8},{10,9... | collective-permute-start | bytes 786440 | tf_op jit(solution)/shard_map/ppermute | solution.py:345
  79.2 16.4 %collective-permute-start.3 = (bf16[2,256,256]{2,1,0:T(8,128)(2,1)}, bf16[2,256,256]{2,1,0:T(8,128)(2,1)}, u32[]{:S(2)}, u32[]{:S(2)}) collective-permute-start(bf16[2,256,256]{2,1,0:T(8,128)(2,1)} %get-tuple-element.19), channel_id=1, source_target_pairs={{0,1},{1,2},{2,3},{3,0},{4,5},{5,6},{6,7},{7,4},{8,9},{9,10},{10,1... | collective-permute-start | bytes 786440 | tf_op jit(solution)/shard_map/ppermute | solution.py:345
  79.3 22.5 %collective-permute-start.4 = (bf16[2,256,256]{2,1,0:T(8,128)(2,1)}, bf16[2,256,256]{2,1,0:T(8,128)(2,1)}, u32[]{:S(2)}, u32[]{:S(2)}) collective-permute-start(bf16[2,256,256]{2,1,0:T(8,128)(2,1)} %get-tuple-element.20), channel_id=1, source_target_pairs={{0,2},{1,3},{2,0},{3,1},{4,6},{5,7},{6,4},{7,5},{8,10},{9,11},{10,... | collective-permute-start | bytes 786440 | tf_op jit(solution)/shard_map/ppermute | solution.py:345
  79.4 24.0 %collective-permute-start.5 = (bf16[2,256,256]{2,1,0:T(8,128)(2,1)}, bf16[2,256,256]{2,1,0:T(8,128)(2,1)}, u32[]{:S(2)}, u32[]{:S(2)}) collective-permute-start(bf16[2,256,256]{2,1,0:T(8,128)(2,1)} %get-tuple-element.21), channel_id=1, source_target_pairs={{0,3},{1,0},{2,1},{3,2},{4,7},{5,4},{6,5},{7,6},{8,11},{9,8},{10,9... | collective-permute-start | bytes 786440 | tf_op jit(solution)/shard_map/ppermute | solution.py:345
  84.1 24.2 %all-to-all-start.3 = ((bf16[8,2,128,256]{3,2,1,0:T(8,128)(2,1)}), bf16[8,2,128,256]{3,2,1,0:T(8,128)(2,1)}, u32[]{:S(2)}, u32[]{:S(2)}) async-start(bf16[8,2,128,256]{3,2,1,0:T(8,128)(2,1)} %roll_planes.1), calls=%async_computation.3 | async-start | bytes 2097152 | tf_op jit(solution)/shard_map/all_to_all | solution.py:339

commit v2 on v1

--- a/solution.py
+++ b/solution.py
@@ -40,14 +40,14 @@
     return lax.dot_general(left, right, (((1,), (0,)), ((), ())), preferred_element_type=jnp.float32)
 
 
-def shift_rows(slots, offset, store, parity):
+def shift_rows(slots, offset, store, parity, scale=1.0):
     count, rows, _ = slots[0].shape
     whole, rest = offset // rows, offset % rows
     to_row = lax.broadcasted_iota(jnp.int32, (rows, 2 * rows), 0)
     if parity:
         to_row = jnp.where(to_row < rows // 2, 2 * to_row, 2 * to_row - (rows - 1))
     from_row = lax.broadcasted_iota(jnp.int32, (rows, 2 * rows), 1)
-    pick = jnp.where(from_row == rows + to_row - rest, 1.0, 0.0).astype(jnp.bfloat16)
+    pick = jnp.where(from_row == rows + to_row - rest, scale, 0.0).astype(jnp.bfloat16)
     for block in range(count):
         here = lax.rem(block - whole + count, count)
         before = lax.rem(block - whole - 1 + 2 * count, count)
@@ -65,6 +65,7 @@
     half_rows = y_rows // halves
     pairs = targets // 2
     factor = 1.0 / math.sqrt(length)
+    assert math.frexp(factor)[0] == 0.5
 
     load = pltpu.make_async_copy(blocks_hbm.at[:, pl.ds(0, 2)], blocks, sems.at[pairs])
     load.start()
@@ -81,7 +82,7 @@
             start = odd * (length // 2) + block * (rows // 2)
             rolled[pl.ds(start, rows // 2), lanes] = values[odd * (rows // 2) : (odd + 1) * (rows // 2)]
 
-    shift_rows([blocks.at[:, part] for part in range(2)], place_ref[0], store, parity=True)
+    shift_rows([blocks.at[:, part] for part in range(2)], place_ref[0], store, parity=True, scale=factor)
 
     def product(step, start):
         both = dot(table[step, :, pl.ds(start, length // 2)], rolled[pl.ds(start, length // 2), :])
@@ -92,11 +93,11 @@
     stores = []
     for step in range(pairs):
         loads[step].wait()
-        sign = jnp.where(lax.rem(place_ref[1] + step, targets) < pairs, factor, -factor)
+        sign = jnp.where(lax.rem(place_ref[1] + step, targets) < pairs, 1.0, -1.0)
         even = product(step, 0)
         odd = product(step, length // 2)
         for part in range(2):
-            from_even, from_odd = even[part] * factor, odd[part] * sign
+            from_even, from_odd = even[part], odd[part] * sign
             pieces[step, part] = (from_even + from_odd).astype(jnp.bfloat16)
             pieces[step + pairs, part] = (from_even - from_odd).astype(jnp.bfloat16)
         for index in (step, step + pairs):
@@ -147,6 +148,7 @@
     tiles, length, tile = table.shape[0], table.shape[1], table.shape[2] // 2
     columns = length // targets
     factor = 1.0 / math.sqrt(length)
+    assert math.frexp(factor)[0] == 0.5
 
     def place_piece(number):
         piece, (behind, row, lane) = pieces[number], layout[number]
@@ -171,7 +173,7 @@
 
     lane = lax.broadcasted_iota(jnp.int32, (columns, columns), 1)
     wanted = jnp.where(lane < columns // 2, 2 * lane, 2 * lane - (columns - 1))
-    pick = jnp.where(lax.broadcasted_iota(jnp.int32, (columns, columns), 0) == wanted, 1.0, 0.0).astype(jnp.bfloat16)
+    pick = jnp.where(lax.broadcasted_iota(jnp.int32, (columns, columns), 0) == wanted, factor, 0.0).astype(jnp.bfloat16)
     for copy in loads:
         copy.wait()
     for source in range(targets):
@@ -190,8 +192,8 @@
         even = product(step, 0)
         odd = product(step, length // 2)
         for part in range(2):
-            out[step, part] = ((even[part] + odd[part]) * factor).astype(jnp.bfloat16)
-            out[step + tiles, part] = ((even[part] - odd[part]) * factor).astype(jnp.bfloat16)
+            out[step, part] = (even[part] + odd[part]).astype(jnp.bfloat16)
+            out[step + tiles, part] = (even[part] - odd[part]).astype(jnp.bfloat16)
         for number in (step, step + tiles):
             stores.append(
                 pltpu.make_async_copy(

time: 111 us -> 111 us (level)
  no operation moved by 1% of the time
where the time goes in v2:
time: 111 us; the launch traced here: 110 us
  Pallas kernels  40.6 us (37%)
  waiting for transfers between devices  34 us (31%)
  starting transfers between devices  32.4 us (29%)
  local copies, waits for them, and re-layouts  1.32 us (1%)
  other arithmetic  1.28 us (1%)
    all_to_all x4, starting transfers between devices, exchange(): return lax.all_to_all(blocks, 'ky', 0, 0, tiled=True)  23.1 us
    ppermute x9, waiting for transfers between devices, along_z(): lax.ppermute(piece, 'kz', [(i, (i + step) % targets) for i in range(targe...  21.8 us
    pallas_call x3, Pallas kernels, z_transform(): pl.pallas_call(functools.partial(z_kernel, layout, targets, component, fi...  14.7 us
    pallas_call x3, Pallas kernels, y_transform(): pl.pallas_call(functools.partial(y_kernel, targets, halves), out_shape=[j...  13.9 us
    all_to_all x4, waiting for transfers between devices, exchange(): return lax.all_to_all(blocks, 'ky', 0, 0, tiled=True)  12.3 us
    ppermute x9, starting transfers between devices, along_z(): lax.ppermute(piece, 'kz', [(i, (i + step) % targets) for i in range(targe...  9.24 us
    pallas_call x4, Pallas kernels, restack(): pl.pallas_call(functools.partial(restack_kernel, steps), out_shape=jax.Sh...  8.58 us
    pallas_call x1, Pallas kernels, roll_planes(): pl.pallas_call(functools.partial(roll_kernel, [number for _, number in sl...  3.31 us
  transfers between devices with their start and end apart: 13, of which 6 were waited for; matrix products, arithmetic and copies ran while one was open for 2% of the time, Pallas kernels for 33%

profile of v2, /device:TPU:11, one launch (start us, length us, event | category | flops | bytes accessed | tf_op | source)
XLA Modules:
  0.0 110.4 jit_solution(10596859478003560581)
XLA Ops:
  0.6 2.0 %by_plane.4 = bf16[8,2,128,256]{3,2,1,0:T(8,128)(2,1)} custom-call(bf16[4,2,8,128,256]{4,3,2,1,0:T(8,128)(2,1)} %from_hbm.5), custom_call_target="tpu_custom_call" | custom-call | tf_op jit(solution)/shard_map/by_plane/pallas_call | solution.py:289
  2.7 5.0 %all-to-all-start.1 = ((bf16[8,2,128,256]{3,2,1,0:T(8,128)(2,1)}), bf16[8,2,128,256]{3,2,1,0:T(8,128)(2,1)}, u32[]{:S(2)}, u32[]{:S(2)}) async-start(bf16[8,2,128,256]{3,2,1,0:T(8,128)(2,1)} %by_plane.4), calls=%async_computation.1 | async-start | bytes 2097152 | tf_op jit(solution)/shard_map/all_to_all | solution.py:341
  7.7 2.0 %by_plane.5 = bf16[8,2,128,256]{3,2,1,0:T(8,128)(2,1)} custom-call(bf16[4,2,8,128,256]{4,3,2,1,0:T(8,128)(2,1)} %from_hbm.5), custom_call_target="tpu_custom_call" | custom-call | tf_op jit(solution)/shard_map/by_plane/pallas_call | solution.py:289
  9.7 2.5 %by_plane.3 = bf16[8,4,128,256]{3,2,1,0:T(8,128)(2,1)} custom-call(bf16[4,2,8,128,256]{4,3,2,1,0:T(8,128)(2,1)} %from_hbm.5), custom_call_target="tpu_custom_call" | custom-call | tf_op jit(solution)/shard_map/by_plane/pallas_call | solution.py:289
  14.8 6.8 %all-to-all-done.1.blocks_hbm = bf16[8,2,128,256]{3,2,1,0:T(8,128)(2,1)} async-done(((bf16[8,2,128,256]{3,2,1,0:T(8,128)(2,1)}), bf16[8,2,128,256]{3,2,1,0:T(8,128)(2,1)}, u32[]{:S(2)}, u32[]{:S(2)}) %all-to-all-start.1) | async-done | bytes 1048608 | tf_op jit(solution)/shard_map/all_to_all | solution.py:341
  21.6 5.7 %all-to-all-start.2 = ((bf16[8,2,128,256]{3,2,1,0:T(8,128)(2,1)}), bf16[8,2,128,256]{3,2,1,0:T(8,128)(2,1)}, u32[]{:S(2)}, u32[]{:S(2)}) async-start(bf16[8,2,128,256]{3,2,1,0:T(8,128)(2,1)} %by_plane.5), calls=%async_computation.2 | async-start | bytes 2097152 | tf_op jit(solution)/shard_map/all_to_all | solution.py:341
  27.3 4.6 %y_transform.3 = (bf16[2,256,256]{2,1,0:T(8,128)(2,1)}, bf16[2,256,256]{2,1,0:T(8,128)(2,1)}, bf16[2,256,256]{2,1,0:T(8,128)(2,1)}, bf16[2,256,256]{2,1,0:T(8,128)(2,1)}) custom-call(s32[2]{0:T(128)} %pad_add_fusion.place_ref, bf16[8,2,128,256]{3,2,1,0:T(8,128)(2,1)} %all-to-all-done.1.blocks_hbm, bf16[2,512,1024]{2,1,0:T(8,128)(2,1)} %constant.17.clone.table_hbm), custom_call_target="tpu_custom_call" | custom-call | flops 40000000000 | tf_op jit(solution)/shard_map/y_transform/pallas_call | solution.py:125
  32.0 1.4 %collective-permute-start = (bf16[2,256,256]{2,1,0:T(8,128)(2,1)}, bf16[2,256,256]{2,1,0:T(8,128)(2,1)}, u32[]{:S(2)}, u32[]{:S(2)}) collective-permute-start(bf16[2,256,256]{2,1,0:T(8,128)(2,1)} %get-tuple-element.15), channel_id=1, source_target_pairs={{0,1},{1,2},{2,3},{3,0},{4,5},{5,6},{6,7},{7,4},{8,9},{9,10},{10,1... | collective-permute-start | bytes 786440 | tf_op jit(solution)/shard_map/ppermute | solution.py:347
  34.4 1.4 %collective-permute-start.2 = (bf16[2,256,256]{2,1,0:T(8,128)(2,1)}, bf16[2,256,256]{2,1,0:T(8,128)(2,1)}, u32[]{:S(2)}, u32[]{:S(2)}) collective-permute-start(bf16[2,256,256]{2,1,0:T(8,128)(2,1)} %get-tuple-element.17), channel_id=1, source_target_pairs={{0,3},{1,0},{2,1},{3,2},{4,7},{5,4},{6,5},{7,6},{8,11},{9,8},{10,9... | collective-permute-start | bytes 786440 | tf_op jit(solution)/shard_map/ppermute | solution.py:347
  35.8 5.4 %all-to-all-done.2.blocks_hbm = bf16[8,2,128,256]{3,2,1,0:T(8,128)(2,1)} async-done(((bf16[8,2,128,256]{3,2,1,0:T(8,128)(2,1)}), bf16[8,2,128,256]{3,2,1,0:T(8,128)(2,1)}, u32[]{:S(2)}, u32[]{:S(2)}) %all-to-all-start.2) | async-done | bytes 1048608 | tf_op jit(solution)/shard_map/all_to_all | solution.py:341
  41.3 5.8 %all-to-all-start = ((bf16[8,4,128,256]{3,2,1,0:T(8,128)(2,1)}), bf16[8,4,128,256]{3,2,1,0:T(8,128)(2,1)}, u32[]{:S(2)}, u32[]{:S(2)}) async-start(bf16[8,4,128,256]{3,2,1,0:T(8,128)(2,1)} %by_plane.3), calls=%async_computation | async-start | bytes 4194304 | tf_op jit(solution)/shard_map/all_to_all | solution.py:341
  47.1 4.7 %y_transform.5 = (bf16[2,256,256]{2,1,0:T(8,128)(2,1)}, bf16[2,256,256]{2,1,0:T(8,128)(2,1)}, bf16[2,256,256]{2,1,0:T(8,128)(2,1)}, bf16[2,256,256]{2,1,0:T(8,128)(2,1)}) custom-call(s32[2]{0:T(128)} %pad_add_fusion.place_ref, bf16[8,2,128,256]{3,2,1,0:T(8,128)(2,1)} %all-to-all-done.2.blocks_hbm, bf16[2,512,1024]{2,1,0:T(8,128)(2,1)} %constant.17.clone.table_hbm), custom_call_target="tpu_custom_call" | custom-call | flops 8000000000 | tf_op jit(solution)/shard_map/y_transform/pallas_call | solution.py:125
  54.2 1.4 %collective-permute-start.8 = (bf16[2,256,256]{2,1,0:T(8,128)(2,1)}, bf16[2,256,256]{2,1,0:T(8,128)(2,1)}, u32[]{:S(2)}, u32[]{:S(2)}) collective-permute-start(bf16[2,256,256]{2,1,0:T(8,128)(2,1)} %get-tuple-element.25), channel_id=1, source_target_pairs={{0,3},{1,0},{2,1},{3,2},{4,7},{5,4},{6,5},{7,6},{8,11},{9,8},{10,9... | collective-permute-start | bytes 786440 | tf_op jit(solution)/shard_map/ppermute | solution.py:347
  55.8 13.8 %collective-permute-done.2.refs_3_ = bf16[2,256,256]{2,1,0:T(8,128)(2,1)} collective-permute-done((bf16[2,256,256]{2,1,0:T(8,128)(2,1)}, bf16[2,256,256]{2,1,0:T(8,128)(2,1)}, u32[]{:S(2)}, u32[]{:S(2)}) %collective-permute-start.2) | collective-permute-done | bytes 262176 | tf_op jit(solution)/shard_map/ppermute | solution.py:347
  69.6 4.9 %z_transform.3.refs_1_.refs_5_ = bf16[3,2,1,256,1024]{4,3,2,1,0:T(8,128)(2,1)} custom-call(s32[2]{0:T(128)} %pad_add_fusion.place_ref, bf16[2,256,256]{2,1,0:T(8,128)(2,1)} %get-tuple-element.14.refs_0_, bf16[2,256,256]{2,1,0:T(8,128)(2,1)} %collective-permute-done.refs_1_, bf16[2,256,256]{2,1,0:T(8,128)(2,1)} %collective-permute-done.1.refs_2_, ...), custom_call_target="tpu_custom_call" | custom-call | flops 40000000000 | tf_op jit(solution)/shard_map/z_transform/pallas_call | solution.py:214
  74.5 4.7 %y_transform.4 = (bf16[2,256,256]{2,1,0:T(8,128)(2,1)}, bf16[2,256,256]{2,1,0:T(8,128)(2,1)}, bf16[2,256,256]{2,1,0:T(8,128)(2,1)}, bf16[2,256,256]{2,1,0:T(8,128)(2,1)}) custom-call(s32[2]{0:T(128)} %pad_add_fusion.place_ref, bf16[8,4,128,256]{3,2,1,0:T(8,128)(2,1)} %after.1.blocks_hbm.refs_0_.refs_1_, bf16[2,512,1024]{2,1,0:T(8,128)(2,1)} %constant.17.clone.table_hbm), custom_call_target="tpu_custom_call" | custom-call | tf_op jit(solution)/shard_map/y_transform/pallas_call | solution.py:125
  79.4 1.4 %collective-permute-start.5 = (bf16[2,256,256]{2,1,0:T(8,128)(2,1)}, bf16[2,256,256]{2,1,0:T(8,128)(2,1)}, u32[]{:S(2)}, u32[]{:S(2)}) collective-permute-start(bf16[2,256,256]{2,1,0:T(8,128)(2,1)} %get-tuple-element.21), channel_id=1, source_target_pairs={{0,3},{1,0},{2,1},{3,2},{4,7},{5,4},{6,5},{7,6},{8,11},{9,8},{10,9... | collective-permute-start | bytes 786440 | tf_op jit(solution)/shard_map/ppermute | solution.py:347
  80.8 3.3 %roll_planes.1 = bf16[8,2,128,256]{3,2,1,0:T(8,128)(2,1)} custom-call(s32[2]{0:T(128)} %pad_add_fusion.place_ref, bf16[8,4,128,256]{3,2,1,0:T(8,128)(2,1)} %after.1.blocks_hbm.refs_0_.refs_1_, bf16[8,4,128,256]{3,2,1,0:T(8,128)(2,1)} %after.1.blocks_hbm.refs_0_.refs_1_), custom_call_target="tpu_custom_call" | custom-call | tf_op jit(solution)/shard_map/roll_planes/pallas_call | solution.py:258
  84.1 6.6 %all-to-all-start.3 = ((bf16[8,2,128,256]{3,2,1,0:T(8,128)(2,1)}), bf16[8,2,128,256]{3,2,1,0:T(8,128)(2,1)}, u32[]{:S(2)}, u32[]{:S(2)}) async-start(bf16[8,2,128,256]{3,2,1,0:T(8,128)(2,1)} %roll_planes.1), calls=%async_computation.3 | async-start | bytes 2097152 | tf_op jit(solution)/shard_map/all_to_all | solution.py:341
  90.7 4.9 %z_transform.4.refs_5_ = bf16[3,2,1,256,1024]{4,3,2,1,0:T(8,128)(2,1)} custom-call(s32[2]{0:T(128)} %pad_add_fusion.place_ref, bf16[2,256,256]{2,1,0:T(8,128)(2,1)} %get-tuple-element.22.refs_0_, bf16[2,256,256]{2,1,0:T(8,128)(2,1)} %collective-permute-done.6.refs_1_, ...), custom_call_target="tpu_custom_call", output_to_operand_aliasing={{}: (6, {})} | custom-call | tf_op jit(solution)/shard_map/z_transform/pallas_call | solution.py:214
  95.6 6.2 %collective-permute-done.4.refs_2_ = bf16[2,256,256]{2,1,0:T(8,128)(2,1)} collective-permute-done((bf16[2,256,256]{2,1,0:T(8,128)(2,1)}, bf16[2,256,256]{2,1,0:T(8,128)(2,1)}, u32[]{:S(2)}, u32[]{:S(2)}) %collective-permute-start.4) | collective-permute-done | bytes 262176 | tf_op jit(solution)/shard_map/ppermute | solution.py:347
  101.8 1.6 %collective-permute-done.5.refs_3_ = bf16[2,256,256]{2,1,0:T(8,128)(2,1)} collective-permute-done((bf16[2,256,256]{2,1,0:T(8,128)(2,1)}, bf16[2,256,256]{2,1,0:T(8,128)(2,1)}, u32[]{:S(2)}, u32[]{:S(2)}) %collective-permute-start.5) | collective-permute-done | bytes 262176 | tf_op jit(solution)/shard_map/ppermute | solution.py:347
  103.4 4.9 %z_transform.5 = bf16[3,2,1,256,1024]{4,3,2,1,0:T(8,128)(2,1)} custom-call(s32[2]{0:T(128)} %pad_add_fusion.place_ref, bf16[2,256,256]{2,1,0:T(8,128)(2,1)} %get-tuple-element.18.refs_0_, bf16[2,256,256]{2,1,0:T(8,128)(2,1)} %collective-permute-done.3.refs_1_, bf16[2,256,256]{2,1,0:T(8,128)(2,1)} %collective-permute-done.4.refs_2_, ...), custom_call_target="tpu_custom_call", output_to_operand_aliasing={{}: (6, {})} | custom-call | flops 40000000000 | tf_op jit(solution)/shard_map/z_transform/pallas_call | solution.py:214
  108.3 2.0 %by_part.1 = bf16[2,8,128,256]{3,2,1,0:T(8,128)(2,1)} custom-call(bf16[8,2,128,256]{3,2,1,0:T(8,128)(2,1)} %all-to-all-done.3.from_hbm), custom_call_target="tpu_custom_call" | custom-call | tf_op jit(solution)/shard_map/by_part/pallas_call | solution.py:289
  (16 shorter events, 6.6 us)
Async XLA Ops:
  2.7 18.9 %all-to-all-start.1 = ((bf16[8,2,128,256]{3,2,1,0:T(8,128)(2,1)}), bf16[8,2,128,256]{3,2,1,0:T(8,128)(2,1)}, u32[]{:S(2)}, u32[]{:S(2)}) async-start(bf16[8,2,128,256]{3,2,1,0:T(8,128)(2,1)} %by_plane.4), calls=%async_computation.1 | async-start | bytes 2097152 | tf_op jit(solution)/shard_map/all_to_all | solution.py:341
  21.6 19.7 %all-to-all-start.2 = ((bf16[8,2,128,256]{3,2,1,0:T(8,128)(2,1)}), bf16[8,2,128,256]{3,2,1,0:T(8,128)(2,1)}, u32[]{:S(2)}, u32[]{:S(2)}) async-start(bf16[8,2,128,256]{3,2,1,0:T(8,128)(2,1)} %by_plane.5), calls=%async_computation.2 | async-start | bytes 2097152 | tf_op jit(solution)/shard_map/all_to_all | solution.py:341
  32.0 22.2 %collective-permute-start = (bf16[2,256,256]{2,1,0:T(8,128)(2,1)}, bf16[2,256,256]{2,1,0:T(8,128)(2,1)}, u32[]{:S(2)}, u32[]{:S(2)}) collective-permute-start(bf16[2,256,256]{2,1,0:T(8,128)(2,1)} %get-tuple-element.15), channel_id=1, source_target_pairs={{0,1},{1,2},{2,3},{3,0},{4,5},{5,6},{6,7},{7,4},{8,9},{9,10},{10,1... | collective-permute-start | bytes 786440 | tf_op jit(solution)/shard_map/ppermute | solution.py:347
  33.3 22.5 %collective-permute-start.1 = (bf16[2,256,256]{2,1,0:T(8,128)(2,1)}, bf16[2,256,256]{2,1,0:T(8,128)(2,1)}, u32[]{:S(2)}, u32[]{:S(2)}) collective-permute-start(bf16[2,256,256]{2,1,0:T(8,128)(2,1)} %get-tuple-element.16), channel_id=1, source_target_pairs={{0,2},{1,3},{2,0},{3,1},{4,6},{5,7},{6,4},{7,5},{8,10},{9,11},{10,... | collective-permute-start | bytes 786440 | tf_op jit(solution)/shard_map/ppermute | solution.py:347
  34.4 35.1 %collective-permute-start.2 = (bf16[2,256,256]{2,1,0:T(8,128)(2,1)}, bf16[2,256,256]{2,1,0:T(8,128)(2,1)}, u32[]{:S(2)}, u32[]{:S(2)}) collective-permute-start(bf16[2,256,256]{2,1,0:T(8,128)(2,1)} %get-tuple-element.17), channel_id=1, source_target_pairs={{0,3},{1,0},{2,1},{3,2},{4,7},{5,4},{6,5},{7,6},{8,11},{9,8},{10,9... | collective-permute-start | bytes 786440 | tf_op jit(solution)/shard_map/ppermute | solution.py:347
  41.3 33.2 %all-to-all-start = ((bf16[8,4,128,256]{3,2,1,0:T(8,128)(2,1)}), bf16[8,4,128,256]{3,2,1,0:T(8,128)(2,1)}, u32[]{:S(2)}, u32[]{:S(2)}) async-start(bf16[8,4,128,256]{3,2,1,0:T(8,128)(2,1)} %by_plane.3), calls=%async_computation | async-start | bytes 4194304 | tf_op jit(solution)/shard_map/all_to_all | solution.py:341
  51.8 27.6 %collective-permute-start.6 = (bf16[2,256,256]{2,1,0:T(8,128)(2,1)}, bf16[2,256,256]{2,1,0:T(8,128)(2,1)}, u32[]{:S(2)}, u32[]{:S(2)}) collective-permute-start(bf16[2,256,256]{2,1,0:T(8,128)(2,1)} %get-tuple-element.23), channel_id=1, source_target_pairs={{0,1},{1,2},{2,3},{3,0},{4,5},{5,6},{6,7},{7,4},{8,9},{9,10},{10,1... | collective-permute-start | bytes 786440 | tf_op jit(solution)/shard_map/ppermute | solution.py:347
  53.1 37.6 %collective-permute-start.7 = (bf16[2,256,256]{2,1,0:T(8,128)(2,1)}, bf16[2,256,256]{2,1,0:T(8,128)(2,1)}, u32[]{:S(2)}, u32[]{:S(2)}) collective-permute-start(bf16[2,256,256]{2,1,0:T(8,128)(2,1)} %get-tuple-element.24), channel_id=1, source_target_pairs={{0,2},{1,3},{2,0},{3,1},{4,6},{5,7},{6,4},{7,5},{8,10},{9,11},{10,... | collective-permute-start | bytes 786440 | tf_op jit(solution)/shard_map/ppermute | solution.py:347
  54.2 36.5 %collective-permute-start.8 = (bf16[2,256,256]{2,1,0:T(8,128)(2,1)}, bf16[2,256,256]{2,1,0:T(8,128)(2,1)}, u32[]{:S(2)}, u32[]{:S(2)}) collective-permute-start(bf16[2,256,256]{2,1,0:T(8,128)(2,1)} %get-tuple-element.25), channel_id=1, source_target_pairs={{0,3},{1,0},{2,1},{3,2},{4,7},{5,4},{6,5},{7,6},{8,11},{9,8},{10,9... | collective-permute-start | bytes 786440 | tf_op jit(solution)/shard_map/ppermute | solution.py:347
  79.2 16.4 %collective-permute-start.3 = (bf16[2,256,256]{2,1,0:T(8,128)(2,1)}, bf16[2,256,256]{2,1,0:T(8,128)(2,1)}, u32[]{:S(2)}, u32[]{:S(2)}) collective-permute-start(bf16[2,256,256]{2,1,0:T(8,128)(2,1)} %get-tuple-element.19), channel_id=1, source_target_pairs={{0,1},{1,2},{2,3},{3,0},{4,5},{5,6},{6,7},{7,4},{8,9},{9,10},{10,1... | collective-permute-start | bytes 786440 | tf_op jit(solution)/shard_map/ppermute | solution.py:347
  79.3 22.5 %collective-permute-start.4 = (bf16[2,256,256]{2,1,0:T(8,128)(2,1)}, bf16[2,256,256]{2,1,0:T(8,128)(2,1)}, u32[]{:S(2)}, u32[]{:S(2)}) collective-permute-start(bf16[2,256,256]{2,1,0:T(8,128)(2,1)} %get-tuple-element.20), channel_id=1, source_target_pairs={{0,2},{1,3},{2,0},{3,1},{4,6},{5,7},{6,4},{7,5},{8,10},{9,11},{10,... | collective-permute-start | bytes 786440 | tf_op jit(solution)/shard_map/ppermute | solution.py:347
  79.4 24.0 %collective-permute-start.5 = (bf16[2,256,256]{2,1,0:T(8,128)(2,1)}, bf16[2,256,256]{2,1,0:T(8,128)(2,1)}, u32[]{:S(2)}, u32[]{:S(2)}) collective-permute-start(bf16[2,256,256]{2,1,0:T(8,128)(2,1)} %get-tuple-element.21), channel_id=1, source_target_pairs={{0,3},{1,0},{2,1},{3,2},{4,7},{5,4},{6,5},{7,6},{8,11},{9,8},{10,9... | collective-permute-start | bytes 786440 | tf_op jit(solution)/shard_map/ppermute | solution.py:347
  84.1 24.2 %all-to-all-start.3 = ((bf16[8,2,128,256]{3,2,1,0:T(8,128)(2,1)}), bf16[8,2,128,256]{3,2,1,0:T(8,128)(2,1)}, u32[]{:S(2)}, u32[]{:S(2)}) async-start(bf16[8,2,128,256]{3,2,1,0:T(8,128)(2,1)} %roll_planes.1), calls=%async_computation.3 | async-start | bytes 2097152 | tf_op jit(solution)/shard_map/all_to_all | solution.py:341

commit v3 on v2

--- a/solution.py
+++ b/solution.py
@@ -226,7 +226,7 @@
             pltpu.SemaphoreType.DMA((2 * tiles,)),
         ],
         input_output_aliases={} if field is None else {len(pieces) + 2: 0},
-        compiler_params=pltpu.CompilerParams(vmem_limit_bytes=VMEM_LIMIT),
+        compiler_params=pltpu.CompilerParams(vmem_limit_bytes=VMEM_LIMIT // 4 if field is not None else VMEM_LIMIT),
         cost_estimate=cost,
         name="z_transform",
     )(place, *pieces, table, *through)
@@ -296,7 +296,7 @@
             pltpu.SemaphoreType.DMA((len(steps),)),
             pltpu.SemaphoreType.DMA((len(steps),)),
         ],
-        compiler_params=pltpu.CompilerParams(vmem_limit_bytes=VMEM_LIMIT),
+        compiler_params=pltpu.CompilerParams(vmem_limit_bytes=VMEM_LIMIT if name == "by_plane" else VMEM_LIMIT // 4),
         cost_estimate=COST,
         name=name,
     )(array)

time: 111 us -> 110 us (level)
  Pallas kernels: 40.6 us -> 38.8 us
where the time goes in v3:
time: 110 us; the launch traced here: 109 us
  Pallas kernels  38.8 us (35%)
  waiting for transfers between devices  34.2 us (31%)
  starting transfers between devices  31.9 us (29%)
  local copies, waits for them, and re-layouts  2.17 us (2%)
  other arithmetic  1.14 us (1%)
    all_to_all x4, starting transfers between devices, exchange(): return lax.all_to_all(blocks, 'ky', 0, 0, tiled=True)  22.6 us
    ppermute x9, waiting for transfers between devices, along_z(): lax.ppermute(piece, 'kz', [(i, (i + step) % targets) for i in range(targe...  21.6 us
    pallas_call x3, Pallas kernels, z_transform(): pl.pallas_call(functools.partial(z_kernel, layout, targets, component, fi...  14 us
    pallas_call x3, Pallas kernels, y_transform(): pl.pallas_call(functools.partial(y_kernel, targets, halves), out_shape=[j...  13.9 us
    all_to_all x4, waiting for transfers between devices, exchange(): return lax.all_to_all(blocks, 'ky', 0, 0, tiled=True)  12.6 us
    ppermute x9, starting transfers between devices, along_z(): lax.ppermute(piece, 'kz', [(i, (i + step) % targets) for i in range(targe...  9.26 us
    pallas_call x4, Pallas kernels, restack(): pl.pallas_call(functools.partial(restack_kernel, steps), out_shape=jax.Sh...  7.59 us
    pallas_call x1, Pallas kernels, roll_planes(): pl.pallas_call(functools.partial(roll_kernel, [number for _, number in sl...  3.32 us
  transfers between devices with their start and end apart: 13, of which 6 were waited for; matrix products, arithmetic and copies ran while one was open for 2% of the time, Pallas kernels for 33%

profile of v3, /device:TPU:11, one launch (start us, length us, event | category | flops | bytes accessed | tf_op | source)
XLA Modules:
  0.0 109.0 jit_solution(15670955277572239902)
XLA Ops:
  0.6 2.0 %by_plane.4 = bf16[8,2,128,256]{3,2,1,0:T(8,128)(2,1)} custom-call(bf16[4,2,8,128,256]{4,3,2,1,0:T(8,128)(2,1)} %from_hbm.5), custom_call_target="tpu_custom_call" | custom-call | tf_op jit(solution)/shard_map/by_plane/pallas_call | solution.py:289
  2.7 5.0 %all-to-all-start.1 = ((bf16[8,2,128,256]{3,2,1,0:T(8,128)(2,1)}), bf16[8,2,128,256]{3,2,1,0:T(8,128)(2,1)}, u32[]{:S(2)}, u32[]{:S(2)}) async-start(bf16[8,2,128,256]{3,2,1,0:T(8,128)(2,1)} %by_plane.4), calls=%async_computation.1 | async-start | bytes 2097152 | tf_op jit(solution)/shard_map/all_to_all | solution.py:341
  7.7 2.0 %by_plane.5 = bf16[8,2,128,256]{3,2,1,0:T(8,128)(2,1)} custom-call(bf16[4,2,8,128,256]{4,3,2,1,0:T(8,128)(2,1)} %from_hbm.5), custom_call_target="tpu_custom_call" | custom-call | tf_op jit(solution)/shard_map/by_plane/pallas_call | solution.py:289
  9.7 2.4 %by_plane.3 = bf16[8,4,128,256]{3,2,1,0:T(8,128)(2,1)} custom-call(bf16[4,2,8,128,256]{4,3,2,1,0:T(8,128)(2,1)} %from_hbm.5), custom_call_target="tpu_custom_call" | custom-call | tf_op jit(solution)/shard_map/by_plane/pallas_call | solution.py:289
  14.5 7.1 %all-to-all-done.1.blocks_hbm = bf16[8,2,128,256]{3,2,1,0:T(8,128)(2,1)} async-done(((bf16[8,2,128,256]{3,2,1,0:T(8,128)(2,1)}), bf16[8,2,128,256]{3,2,1,0:T(8,128)(2,1)}, u32[]{:S(2)}, u32[]{:S(2)}) %all-to-all-start.1) | async-done | bytes 1048608 | tf_op jit(solution)/shard_map/all_to_all | solution.py:341
  21.6 5.7 %all-to-all-start.2 = ((bf16[8,2,128,256]{3,2,1,0:T(8,128)(2,1)}), bf16[8,2,128,256]{3,2,1,0:T(8,128)(2,1)}, u32[]{:S(2)}, u32[]{:S(2)}) async-start(bf16[8,2,128,256]{3,2,1,0:T(8,128)(2,1)} %by_plane.5), calls=%async_computation.2 | async-start | bytes 2097152 | tf_op jit(solution)/shard_map/all_to_all | solution.py:341
  27.3 4.6 %y_transform.3 = (bf16[2,256,256]{2,1,0:T(8,128)(2,1)}, bf16[2,256,256]{2,1,0:T(8,128)(2,1)}, bf16[2,256,256]{2,1,0:T(8,128)(2,1)}, bf16[2,256,256]{2,1,0:T(8,128)(2,1)}) custom-call(s32[2]{0:T(128)} %pad_add_fusion.place_ref, bf16[8,2,128,256]{3,2,1,0:T(8,128)(2,1)} %all-to-all-done.1.blocks_hbm, bf16[2,512,1024]{2,1,0:T(8,128)(2,1)} %constant.17.clone.table_hbm), custom_call_target="tpu_custom_call" | custom-call | flops 40000000000 | tf_op jit(solution)/shard_map/y_transform/pallas_call | solution.py:125
  32.0 1.3 %collective-permute-start = (bf16[2,256,256]{2,1,0:T(8,128)(2,1)}, bf16[2,256,256]{2,1,0:T(8,128)(2,1)}, u32[]{:S(2)}, u32[]{:S(2)}) collective-permute-start(bf16[2,256,256]{2,1,0:T(8,128)(2,1)} %get-tuple-element.15), channel_id=1, source_target_pairs={{0,1},{1,2},{2,3},{3,0},{4,5},{5,6},{6,7},{7,4},{8,9},{9,10},{10,1... | collective-permute-start | bytes 786440 | tf_op jit(solution)/shard_map/ppermute | solution.py:347
  34.4 1.4 %collective-permute-start.2 = (bf16[2,256,256]{2,1,0:T(8,128)(2,1)}, bf16[2,256,256]{2,1,0:T(8,128)(2,1)}, u32[]{:S(2)}, u32[]{:S(2)}) collective-permute-start(bf16[2,256,256]{2,1,0:T(8,128)(2,1)} %get-tuple-element.17), channel_id=1, source_target_pairs={{0,3},{1,0},{2,1},{3,2},{4,7},{5,4},{6,5},{7,6},{8,11},{9,8},{10,9... | collective-permute-start | bytes 786440 | tf_op jit(solution)/shard_map/ppermute | solution.py:347
  35.8 5.5 %all-to-all-done.2.blocks_hbm = bf16[8,2,128,256]{3,2,1,0:T(8,128)(2,1)} async-done(((bf16[8,2,128,256]{3,2,1,0:T(8,128)(2,1)}), bf16[8,2,128,256]{3,2,1,0:T(8,128)(2,1)}, u32[]{:S(2)}, u32[]{:S(2)}) %all-to-all-start.2) | async-done | bytes 1048608 | tf_op jit(solution)/shard_map/all_to_all | solution.py:341
  41.3 5.8 %all-to-all-start = ((bf16[8,4,128,256]{3,2,1,0:T(8,128)(2,1)}), bf16[8,4,128,256]{3,2,1,0:T(8,128)(2,1)}, u32[]{:S(2)}, u32[]{:S(2)}) async-start(bf16[8,4,128,256]{3,2,1,0:T(8,128)(2,1)} %by_plane.3), calls=%async_computation | async-start | bytes 4194304 | tf_op jit(solution)/shard_map/all_to_all | solution.py:341
  47.1 4.6 %y_transform.5 = (bf16[2,256,256]{2,1,0:T(8,128)(2,1)}, bf16[2,256,256]{2,1,0:T(8,128)(2,1)}, bf16[2,256,256]{2,1,0:T(8,128)(2,1)}, bf16[2,256,256]{2,1,0:T(8,128)(2,1)}) custom-call(s32[2]{0:T(128)} %pad_add_fusion.place_ref, bf16[8,2,128,256]{3,2,1,0:T(8,128)(2,1)} %all-to-all-done.2.blocks_hbm, bf16[2,512,1024]{2,1,0:T(8,128)(2,1)} %constant.17.clone.table_hbm), custom_call_target="tpu_custom_call" | custom-call | flops 8000000000 | tf_op jit(solution)/shard_map/y_transform/pallas_call | solution.py:125
  51.8 1.3 %collective-permute-start.6 = (bf16[2,256,256]{2,1,0:T(8,128)(2,1)}, bf16[2,256,256]{2,1,0:T(8,128)(2,1)}, u32[]{:S(2)}, u32[]{:S(2)}) collective-permute-start(bf16[2,256,256]{2,1,0:T(8,128)(2,1)} %get-tuple-element.23), channel_id=1, source_target_pairs={{0,1},{1,2},{2,3},{3,0},{4,5},{5,6},{6,7},{7,4},{8,9},{9,10},{10,1... | collective-permute-start | bytes 786440 | tf_op jit(solution)/shard_map/ppermute | solution.py:347
  54.2 1.4 %collective-permute-start.8 = (bf16[2,256,256]{2,1,0:T(8,128)(2,1)}, bf16[2,256,256]{2,1,0:T(8,128)(2,1)}, u32[]{:S(2)}, u32[]{:S(2)}) collective-permute-start(bf16[2,256,256]{2,1,0:T(8,128)(2,1)} %get-tuple-element.25), channel_id=1, source_target_pairs={{0,3},{1,0},{2,1},{3,2},{4,7},{5,4},{6,5},{7,6},{8,11},{9,8},{10,9... | collective-permute-start | bytes 786440 | tf_op jit(solution)/shard_map/ppermute | solution.py:347
  55.8 13.7 %collective-permute-done.2.refs_3_ = bf16[2,256,256]{2,1,0:T(8,128)(2,1)} collective-permute-done((bf16[2,256,256]{2,1,0:T(8,128)(2,1)}, bf16[2,256,256]{2,1,0:T(8,128)(2,1)}, u32[]{:S(2)}, u32[]{:S(2)}) %collective-permute-start.2) | collective-permute-done | bytes 262176 | tf_op jit(solution)/shard_map/ppermute | solution.py:347
  69.6 4.9 %z_transform.3.refs_1_.refs_5_ = bf16[3,2,1,256,1024]{4,3,2,1,0:T(8,128)(2,1)} custom-call(s32[2]{0:T(128)} %pad_add_fusion.place_ref, bf16[2,256,256]{2,1,0:T(8,128)(2,1)} %get-tuple-element.14.refs_0_, bf16[2,256,256]{2,1,0:T(8,128)(2,1)} %collective-permute-done.refs_1_, bf16[2,256,256]{2,1,0:T(8,128)(2,1)} %collective-permute-done.1.refs_2_, ...), custom_call_target="tpu_custom_call" | custom-call | flops 40000000000 | tf_op jit(solution)/shard_map/z_transform/pallas_call | solution.py:214
  74.5 4.6 %y_transform.4 = (bf16[2,256,256]{2,1,0:T(8,128)(2,1)}, bf16[2,256,256]{2,1,0:T(8,128)(2,1)}, bf16[2,256,256]{2,1,0:T(8,128)(2,1)}, bf16[2,256,256]{2,1,0:T(8,128)(2,1)}) custom-call(s32[2]{0:T(128)} %pad_add_fusion.place_ref, bf16[8,4,128,256]{3,2,1,0:T(8,128)(2,1)} %after.1.blocks_hbm.refs_0_.refs_1_, bf16[2,512,1024]{2,1,0:T(8,128)(2,1)} %constant.17.clone.table_hbm), custom_call_target="tpu_custom_call" | custom-call | tf_op jit(solution)/shard_map/y_transform/pallas_call | solution.py:125
  79.4 1.4 %collective-permute-start.5 = (bf16[2,256,256]{2,1,0:T(8,128)(2,1)}, bf16[2,256,256]{2,1,0:T(8,128)(2,1)}, u32[]{:S(2)}, u32[]{:S(2)}) collective-permute-start(bf16[2,256,256]{2,1,0:T(8,128)(2,1)} %get-tuple-element.21), channel_id=1, source_target_pairs={{0,3},{1,0},{2,1},{3,2},{4,7},{5,4},{6,5},{7,6},{8,11},{9,8},{10,9... | collective-permute-start | bytes 786440 | tf_op jit(solution)/shard_map/ppermute | solution.py:347
  80.8 3.3 %roll_planes.1 = bf16[8,2,128,256]{3,2,1,0:T(8,128)(2,1)} custom-call(s32[2]{0:T(128)} %pad_add_fusion.place_ref, bf16[8,4,128,256]{3,2,1,0:T(8,128)(2,1)} %after.1.blocks_hbm.refs_0_.refs_1_, bf16[8,4,128,256]{3,2,1,0:T(8,128)(2,1)} %after.1.blocks_hbm.refs_0_.refs_1_), custom_call_target="tpu_custom_call" | custom-call | tf_op jit(solution)/shard_map/roll_planes/pallas_call | solution.py:258
  84.1 6.0 %all-to-all-start.3 = ((bf16[8,2,128,256]{3,2,1,0:T(8,128)(2,1)}), bf16[8,2,128,256]{3,2,1,0:T(8,128)(2,1)S(1)}, u32[]{:S(2)}, u32[]{:S(2)}) async-start(bf16[8,2,128,256]{3,2,1,0:T(8,128)(2,1)} %roll_planes.1), calls=%async_computation.3 | async-start | bytes 2097152 | tf_op jit(solution)/shard_map/all_to_all | solution.py:341
  91.1 4.5 %z_transform.4.refs_5_ = bf16[3,2,1,256,1024]{4,3,2,1,0:T(8,128)(2,1)} custom-call(s32[2]{0:T(128)S(1)} %copy-done.2, bf16[2,256,256]{2,1,0:T(8,128)(2,1)S(1)} %copy-done.1, bf16[2,256,256]{2,1,0:T(8,128)(2,1)} %collective-permute-done.6.refs_1_, bf16[2,256,256]{2,1,0:T(8,128)(2,1)} %collective-permute-done.7.refs_2_, ...), custom_call_target="tpu_custom_call", output_to_operand_aliasing={{}: (6, {})} | custom-call | tf_op jit(solution)/shard_map/z_transform/pallas_call | solution.py:214
  95.7 6.1 %collective-permute-done.4.refs_2_ = bf16[2,256,256]{2,1,0:T(8,128)(2,1)} collective-permute-done((bf16[2,256,256]{2,1,0:T(8,128)(2,1)}, bf16[2,256,256]{2,1,0:T(8,128)(2,1)}, u32[]{:S(2)}, u32[]{:S(2)}) %collective-permute-start.4) | collective-permute-done | bytes 262176 | tf_op jit(solution)/shard_map/ppermute | solution.py:347
  101.8 1.5 %collective-permute-done.5.refs_3_ = bf16[2,256,256]{2,1,0:T(8,128)(2,1)} collective-permute-done((bf16[2,256,256]{2,1,0:T(8,128)(2,1)}, bf16[2,256,256]{2,1,0:T(8,128)(2,1)}, u32[]{:S(2)}, u32[]{:S(2)}) %collective-permute-start.5) | collective-permute-done | bytes 262176 | tf_op jit(solution)/shard_map/ppermute | solution.py:347
  103.3 4.5 %z_transform.5 = bf16[3,2,1,256,1024]{4,3,2,1,0:T(8,128)(2,1)} custom-call(s32[2]{0:T(128)S(1)} %copy-done.2, bf16[2,256,256]{2,1,0:T(8,128)(2,1)S(1)} %copy-done.3, bf16[2,256,256]{2,1,0:T(8,128)(2,1)} %collective-permute-done.3.refs_1_, bf16[2,256,256]{2,1,0:T(8,128)(2,1)} %collective-permute-done.4.refs_2_, ...), custom_call_target="tpu_custom_call", output_to_operand_aliasing={{}: (6, {})} | custom-call | flops 40000000000 | tf_op jit(solution)/shard_map/z_transform/pallas_call | solution.py:214
  (24 shorter events, 7.1 us)
Async XLA Ops:
  2.7 18.9 %all-to-all-start.1 = ((bf16[8,2,128,256]{3,2,1,0:T(8,128)(2,1)}), bf16[8,2,128,256]{3,2,1,0:T(8,128)(2,1)}, u32[]{:S(2)}, u32[]{:S(2)}) async-start(bf16[8,2,128,256]{3,2,1,0:T(8,128)(2,1)} %by_plane.4), calls=%async_computation.1 | async-start | bytes 2097152 | tf_op jit(solution)/shard_map/all_to_all | solution.py:341
  21.6 19.7 %all-to-all-start.2 = ((bf16[8,2,128,256]{3,2,1,0:T(8,128)(2,1)}), bf16[8,2,128,256]{3,2,1,0:T(8,128)(2,1)}, u32[]{:S(2)}, u32[]{:S(2)}) async-start(bf16[8,2,128,256]{3,2,1,0:T(8,128)(2,1)} %by_plane.5), calls=%async_computation.2 | async-start | bytes 2097152 | tf_op jit(solution)/shard_map/all_to_all | solution.py:341
  32.0 22.2 %collective-permute-start = (bf16[2,256,256]{2,1,0:T(8,128)(2,1)}, bf16[2,256,256]{2,1,0:T(8,128)(2,1)}, u32[]{:S(2)}, u32[]{:S(2)}) collective-permute-start(bf16[2,256,256]{2,1,0:T(8,128)(2,1)} %get-tuple-element.15), channel_id=1, source_target_pairs={{0,1},{1,2},{2,3},{3,0},{4,5},{5,6},{6,7},{7,4},{8,9},{9,10},{10,1... | collective-permute-start | bytes 786440 | tf_op jit(solution)/shard_map/ppermute | solution.py:347
  33.3 22.5 %collective-permute-start.1 = (bf16[2,256,256]{2,1,0:T(8,128)(2,1)}, bf16[2,256,256]{2,1,0:T(8,128)(2,1)}, u32[]{:S(2)}, u32[]{:S(2)}) collective-permute-start(bf16[2,256,256]{2,1,0:T(8,128)(2,1)} %get-tuple-element.16), channel_id=1, source_target_pairs={{0,2},{1,3},{2,0},{3,1},{4,6},{5,7},{6,4},{7,5},{8,10},{9,11},{10,... | collective-permute-start | bytes 786440 | tf_op jit(solution)/shard_map/ppermute | solution.py:347
  34.4 35.1 %collective-permute-start.2 = (bf16[2,256,256]{2,1,0:T(8,128)(2,1)}, bf16[2,256,256]{2,1,0:T(8,128)(2,1)}, u32[]{:S(2)}, u32[]{:S(2)}) collective-permute-start(bf16[2,256,256]{2,1,0:T(8,128)(2,1)} %get-tuple-element.17), channel_id=1, source_target_pairs={{0,3},{1,0},{2,1},{3,2},{4,7},{5,4},{6,5},{7,6},{8,11},{9,8},{10,9... | collective-permute-start | bytes 786440 | tf_op jit(solution)/shard_map/ppermute | solution.py:347
  41.3 33.2 %all-to-all-start = ((bf16[8,4,128,256]{3,2,1,0:T(8,128)(2,1)}), bf16[8,4,128,256]{3,2,1,0:T(8,128)(2,1)}, u32[]{:S(2)}, u32[]{:S(2)}) async-start(bf16[8,4,128,256]{3,2,1,0:T(8,128)(2,1)} %by_plane.3), calls=%async_computation | async-start | bytes 4194304 | tf_op jit(solution)/shard_map/all_to_all | solution.py:341
  51.8 27.6 %collective-permute-start.6 = (bf16[2,256,256]{2,1,0:T(8,128)(2,1)}, bf16[2,256,256]{2,1,0:T(8,128)(2,1)}, u32[]{:S(2)}, u32[]{:S(2)}) collective-permute-start(bf16[2,256,256]{2,1,0:T(8,128)(2,1)} %get-tuple-element.23), channel_id=1, source_target_pairs={{0,1},{1,2},{2,3},{3,0},{4,5},{5,6},{6,7},{7,4},{8,9},{9,10},{10,1... | collective-permute-start | bytes 786440 | tf_op jit(solution)/shard_map/ppermute | solution.py:347
  53.1 37.0 %collective-permute-start.7 = (bf16[2,256,256]{2,1,0:T(8,128)(2,1)}, bf16[2,256,256]{2,1,0:T(8,128)(2,1)}, u32[]{:S(2)}, u32[]{:S(2)}) collective-permute-start(bf16[2,256,256]{2,1,0:T(8,128)(2,1)} %get-tuple-element.24), channel_id=1, source_target_pairs={{0,2},{1,3},{2,0},{3,1},{4,6},{5,7},{6,4},{7,5},{8,10},{9,11},{10,... | collective-permute-start | bytes 786440 | tf_op jit(solution)/shard_map/ppermute | solution.py:347
  54.2 35.9 %collective-permute-start.8 = (bf16[2,256,256]{2,1,0:T(8,128)(2,1)}, bf16[2,256,256]{2,1,0:T(8,128)(2,1)}, u32[]{:S(2)}, u32[]{:S(2)}) collective-permute-start(bf16[2,256,256]{2,1,0:T(8,128)(2,1)} %get-tuple-element.25), channel_id=1, source_target_pairs={{0,3},{1,0},{2,1},{3,2},{4,7},{5,4},{6,5},{7,6},{8,11},{9,8},{10,9... | collective-permute-start | bytes 786440 | tf_op jit(solution)/shard_map/ppermute | solution.py:347
  79.1 16.5 %collective-permute-start.3 = (bf16[2,256,256]{2,1,0:T(8,128)(2,1)}, bf16[2,256,256]{2,1,0:T(8,128)(2,1)}, u32[]{:S(2)}, u32[]{:S(2)}) collective-permute-start(bf16[2,256,256]{2,1,0:T(8,128)(2,1)} %get-tuple-element.19), channel_id=1, source_target_pairs={{0,1},{1,2},{2,3},{3,0},{4,5},{5,6},{6,7},{7,4},{8,9},{9,10},{10,1... | collective-permute-start | bytes 786440 | tf_op jit(solution)/shard_map/ppermute | solution.py:347
  79.2 22.6 %collective-permute-start.4 = (bf16[2,256,256]{2,1,0:T(8,128)(2,1)}, bf16[2,256,256]{2,1,0:T(8,128)(2,1)}, u32[]{:S(2)}, u32[]{:S(2)}) collective-permute-start(bf16[2,256,256]{2,1,0:T(8,128)(2,1)} %get-tuple-element.20), channel_id=1, source_target_pairs={{0,2},{1,3},{2,0},{3,1},{4,6},{5,7},{6,4},{7,5},{8,10},{9,11},{10,... | collective-permute-start | bytes 786440 | tf_op jit(solution)/shard_map/ppermute | solution.py:347
  79.4 24.0 %collective-permute-start.5 = (bf16[2,256,256]{2,1,0:T(8,128)(2,1)}, bf16[2,256,256]{2,1,0:T(8,128)(2,1)}, u32[]{:S(2)}, u32[]{:S(2)}) collective-permute-start(bf16[2,256,256]{2,1,0:T(8,128)(2,1)} %get-tuple-element.21), channel_id=1, source_target_pairs={{0,3},{1,0},{2,1},{3,2},{4,7},{5,4},{6,5},{7,6},{8,11},{9,8},{10,9... | collective-permute-start | bytes 786440 | tf_op jit(solution)/shard_map/ppermute | solution.py:347
  84.1 6.1 %copy-start = (bf16[2,1024,512]{2,1,0:T(8,128)(2,1)S(1)}, bf16[2,1024,512]{2,1,0:T(8,128)(2,1)}, u32[]{:S(2)}) copy-start(bf16[2,1024,512]{2,1,0:T(8,128)(2,1)} %constant.18.clone.refs_4_) | copy-start | bytes 6291460
  84.1 6.1 %copy-start.2 = (s32[2]{0:T(128)S(1)}, s32[2]{0:T(128)}, u32[]{:S(2)}) copy-start(s32[2]{0:T(128)} %pad_add_fusion.place_ref) | copy-start | bytes 28
  84.1 23.8 %all-to-all-start.3 = ((bf16[8,2,128,256]{3,2,1,0:T(8,128)(2,1)}), bf16[8,2,128,256]{3,2,1,0:T(8,128)(2,1)S(1)}, u32[]{:S(2)}, u32[]{:S(2)}) async-start(bf16[8,2,128,256]{3,2,1,0:T(8,128)(2,1)} %roll_planes.1), calls=%async_computation.3 | async-start | bytes 2097152 | tf_op jit(solution)/shard_map/all_to_all | solution.py:341
  90.2 1.0 copy-start.1
  91.1 12.2 %copy-start.3 = (bf16[2,256,256]{2,1,0:T(8,128)(2,1)S(1)}, bf16[2,256,256]{2,1,0:T(8,128)(2,1)}, u32[]{:S(2)}) copy-start(bf16[2,256,256]{2,1,0:T(8,128)(2,1)} %get-tuple-element.18.refs_0_) | copy-start | bytes 786436
